TPU v7x, 128 devices: a whole 4x4x4 slice. The times are simulated.
128 devices in a mesh: dp: 8 (over z_lo, y), ctx: 16 (over z_hi, x, core).
Axes of the slice: x: 4, y: 4, z: 4 (z_hi: 2, z_lo: 2; z = z_hi * 2 + z_lo), core: 2. Of those that a mesh axis runs over, the one named last changes fastest.
Arguments:
- inputs: bfloat16 [16384, 2048], P(('dp', 'ctx')), may hold values from -6 to 6
- positions: int32 [16384], P(('dp', 'ctx')), may hold values from 0 to 1919, as said below
- cotangent: bfloat16 [16384, 2048], P(('dp', 'ctx')), may hold values from -6 to 6
- w_query: bfloat16 [2048, 2048], P('dp'), may hold values from -0.125 to 0.125
- w_key: bfloat16 [2048, 256], P('dp'), may hold values from -0.125 to 0.125
- w_value: bfloat16 [2048, 256], P('dp'), may hold values from -0.125 to 0.125
- w_out: bfloat16 [2048, 2048], P('dp'), may hold values from -0.75 to 0.75
- w_gate: bfloat16 [2048, 5632], P('dp'), may hold values from -0.125 to 0.125
- w_up: bfloat16 [2048, 5632], P('dp'), may hold values from -0.125 to 0.125
- w_down: bfloat16 [5632, 2048], P('dp'), may hold values from -0.15625 to 0.15625
- gain_attn: bfloat16 [2048], P('dp'), may hold values from 0.25 to 1.75
- gain_mlp: bfloat16 [2048], P('dp'), may hold values from 0.25 to 1.75
Outputs:
- output: bfloat16 [16384, 2048], P(('dp', 'ctx'))
- grad_inputs: float32 [16384, 2048], P(('dp', 'ctx'))
- grad_query: float32 [2048, 2048], P('dp')
- grad_key: float32 [2048, 256], P('dp')
- grad_value: float32 [2048, 256], P('dp')
- grad_out: float32 [2048, 2048], P('dp')
- grad_gate: float32 [2048, 5632], P('dp')
- grad_up: float32 [2048, 5632], P('dp')
- grad_down: float32 [5632, 2048], P('dp')
- grad_gain_attn: float32 [2048], P('dp')
- grad_gain_mlp: float32 [2048], P('dp')
Inputs may be any that keep to these rules, and one draw needn't show every extreme that they name: Within each sequence positions count up from 0 inside three contiguous documents: a first one begins the sequence and ends inside its first 128 tokens, a second one of exactly 1920 tokens follows it, and a third one fills the rest.
All inputs are finite; a program needn't handle non-finite values.
Results may differ from a plain program's by a relative error of at most 0.03.
Values may be sent and summed in bfloat16 or wider, within the bound.
No kernel may reach another device: no remote copies, remote signals or barrier semaphores. Data moves between devices by JAX's collectives and lax.ppermute only.
A program may use at most 320 MiB of HBM per device.

v0:
```python
import functools
import math

import jax
import jax.numpy as jnp
from jax import lax
from jax.experimental import pallas as pl
from jax.experimental.pallas import tpu as pltpu
from jax.sharding import Mesh, PartitionSpec as P

D = 2048
HEADS = 32
KV_HEADS = 4
HEAD_DIM = 64
FF = 5632
LENGTH = 2048
MIDDLE = 1920
EPSILON = 1e-05
THETA = 10000.0
NEG_LARGE = -1e30

AXES = ("zl", "y", "zh", "x", "core")
Z_RING = ("zl", "zh")
GROUP = 8
TOK = 128
HALF = GROUP * TOK
CHUNK = D // GROUP
FF_OWN = FF // GROUP
Q_OWN = HEADS * HEAD_DIM // GROUP
HEADS_OWN = HEADS // GROUP
SUB = FF_OWN // GROUP
OUT_SUB = Q_OWN // GROUP
KEY_CHUNK = 256
ROWS_Q = HEADS_OWN * TOK

F32 = jnp.float32
BF16 = jnp.bfloat16


def ring(values, axis, step):
    if axis == Z_RING:
        spot = [(z % 2) * 2 + z // 2 for z in range(4)]
        return lax.ppermute(values, axis, [(spot[z], spot[(z + step) % 4]) for z in range(4)])
    count = lax.axis_size(axis)
    return lax.ppermute(values, axis, [(i, (i + step) % count) for i in range(count)])


def place_kernel(copies, places, *refs):
    pieces, out, sems = refs[:-2], refs[-2], refs[-1]
    running = [
        pltpu.make_async_copy(
            pieces[piece].at[pl.ds(start, count)], out.at[pl.ds(places[i], count)], sems.at[i]
        )
        for i, (piece, start, count) in enumerate(copies)
    ]
    for copy in running:
        copy.start()
    for copy in running:
        copy.wait()


def cost(microseconds):
    return pl.CostEstimate(
        flops=int(microseconds * 1e9), bytes_accessed=int(microseconds * 3e6), transcendentals=0
    )


def put_in_place(places, pieces, copies, total):
    return pl.pallas_call(
        functools.partial(place_kernel, copies),
        grid_spec=pltpu.PrefetchScalarGridSpec(
            num_scalar_prefetch=1,
            grid=(1,),
            in_specs=[pl.BlockSpec(piece.shape, lambda i, places: (0, 0, 0)) for piece in pieces],
            out_specs=pl.BlockSpec(memory_space=pl.ANY),
            scratch_shapes=[pltpu.SemaphoreType.DMA((len(copies),))],
        ),
        out_shape=jax.ShapeDtypeStruct((total, *pieces[0].shape[1:]), pieces[0].dtype),
        compiler_params=pltpu.CompilerParams(vmem_limit_bytes=32 * 1024 * 1024),
        cost_estimate=cost(1),
        name="put_in_place",
    )(places, *pieces)


def near(block, axis):
    return ring(block, axis, -1), ring(block, axis, 1)


def far(ahead, behind, axis):
    half = ahead.shape[0] // 2
    return ring(ahead[:half], axis, -1), ring(behind[half:], axis, 1)


def across_z(own, ahead, behind, far_low, far_high):
    return (
        ring(jnp.concatenate([own, ahead]), Z_RING, 1),
        ring(jnp.concatenate([behind, far_low, far_high]), Z_RING, -1),
    )


def put_weights(blocks, z_blocks, zl, y):
    rows, columns = blocks[0].shape
    unit = rows // 2
    pieces = [block.reshape(-1, unit, columns) for block in (*blocks, *z_blocks)]
    copies = [(0, 0, 2), (1, 0, 2), (2, 0, 2), (3, 0, 1), (4, 0, 1)]
    copies += [(5, 0, 2), (5, 2, 2), (6, 0, 2), (6, 2, 2)]
    step = [(y + q) % 4 * 2 for q in range(4)]
    mine, other = zl * 8, (1 - zl) * 8
    places = [mine + step[0], mine + step[1], mine + step[3], mine + step[2], mine + step[2] + 1]
    places += [other + step[0], other + step[1], other + step[3], other + step[2]]
    places = jnp.stack(places).astype(jnp.int32)
    return put_in_place(places, pieces, copies, 16).reshape(8 * rows, columns)


def halves_kernel(copies, places, *refs):
    pieces, out, sems = refs[:-2], refs[-2], refs[-1]
    width = pieces[0].shape[-1]
    running = [
        pltpu.make_async_copy(
            pieces[piece].at[unit],
            out.at[places[i], :, pl.ds(unit % 2 * width, width)],
            sems.at[i],
        )
        for i, (piece, unit) in enumerate(copies)
    ]
    for copy in running:
        copy.start()
    for copy in running:
        copy.wait()


def stack_halves(block):
    half = block.shape[1] // 2
    return jnp.concatenate([block[:, :half], block[:, half:]])


def both_parities(own):
    half = own.shape[0] // 2
    return ring(own[:half], Z_RING, 1), ring(own[half:], Z_RING, -1)


def pair_places(zl, y):
    steps = [(y + q) % 4 for q in (0, 1, 3, 2)]
    return [[zl * 4 + at, (1 - zl) * 4 + at] for at in steps]


def put_pairs(pair, near_pairs, far_pair, zl, y):
    rows, columns = far_pair[0].shape
    pieces = [block.reshape(-1, rows, columns) for block in (pair, *near_pairs, *far_pair)]
    copies = [(i, u, 1) for i in range(3) for u in range(2)] + [(3, 0, 1), (4, 0, 1)]
    places = jnp.stack(sum(pair_places(zl, y), [])).astype(jnp.int32)
    return put_in_place(places, pieces, copies, 8).reshape(8 * rows, columns)


def put_row_pairs(pair, near_pairs, far_pair, zl, y):
    rows, columns = far_pair[0].shape
    unit = rows // 2
    pieces = [block.reshape(-1, unit, columns) for block in (pair, *near_pairs, *far_pair)]
    copies = [(i, u) for i in range(3) for u in range(4)]
    copies += [(i, u) for i in (3, 4) for u in range(2)]
    places = sum([[at, at] for spots in pair_places(zl, y) for at in spots], [])
    places = jnp.stack(places).astype(jnp.int32)
    return pl.pallas_call(
        functools.partial(halves_kernel, copies),
        grid_spec=pltpu.PrefetchScalarGridSpec(
            num_scalar_prefetch=1,
            grid=(1,),
            in_specs=[pl.BlockSpec(piece.shape, lambda i, places: (0, 0, 0)) for piece in pieces],
            out_specs=pl.BlockSpec(memory_space=pl.ANY),
            scratch_shapes=[pltpu.SemaphoreType.DMA((len(copies),))],
        ),
        out_shape=jax.ShapeDtypeStruct((8, unit, 2 * columns), BF16),
        compiler_params=pltpu.CompilerParams(vmem_limit_bytes=32 * 1024 * 1024),
        cost_estimate=cost(1),
        name="put_rows",
    )(places, *pieces).reshape(8 * unit, 2 * columns)


def put_rows(blocks, blocks_two, group_places):
    rows, columns = blocks[0].shape
    unit = rows // 2
    pieces = [block.reshape(-1, unit, columns) for block in (*blocks, *blocks_two)]
    copies = [(0, 0, 2), (1, 0, 2), (2, 0, 2), (3, 0, 1), (4, 0, 1)]
    copies += [(5, 0, 2), (6, 0, 2), (6, 2, 2), (7, 0, 2)]
    spots = [2 * group_places[i] for i in (0, 1, 3, 2, 2, 4, 5, 7, 6)]
    spots[4] = spots[4] + 1
    return put_in_place(jnp.stack(spots), pieces, copies, 2 * GROUP).reshape(
        GROUP * rows, columns
    )


def swap_blocks(own, ahead, behind, far_low, far_high):
    return (
        ring(own, "core", 1),
        ring(jnp.concatenate([ahead, behind]), "core", 1),
        ring(jnp.concatenate([far_low, far_high]), "core", 1),
    )


def scatter_z(pairs):
    return ring(pairs[0], Z_RING, 1), ring(pairs[1], Z_RING, -1)


def chunk_for_y(own, arrived, y, step):
    at = (y + step) % 4
    more = jnp.where(
        at < 2,
        lax.dynamic_index_in_dim(arrived[0], at & 1, 0, keepdims=False),
        lax.dynamic_index_in_dim(arrived[1], at & 1, 0, keepdims=False),
    )
    here = lax.dynamic_index_in_dim(own, at, 0, keepdims=False)
    return here.astype(F32) + more.astype(F32)


def chunks_for_y(own, arrived, y):
    return [chunk_for_y(own, arrived, y, 0)] + [
        chunk_for_y(own, arrived, y, step).astype(BF16) for step in (1, 2, 3)
    ]


def far_along_y(own, arrived, y):
    block = chunk_for_y(own, arrived, y, 2).astype(BF16)
    half = block.shape[0] // 2
    return ring(block[:half], "y", 1), ring(block[half:], "y", -1)


def near_along_y(own, arrived, first, y):
    ahead, behind = chunk_for_y(own, arrived, y, 1), chunk_for_y(own, arrived, y, 3)
    half = ahead.shape[0] // 2
    ahead = jnp.concatenate([ahead[:half] + first[0].astype(F32), ahead[half:]])
    behind = jnp.concatenate([behind[:half], behind[half:] + first[1].astype(F32)])
    return (
        chunk_for_y(own, arrived, y, 0),
        ring(ahead.astype(BF16), "y", 1),
        ring(behind.astype(BF16), "y", -1),
    )


def send_along_y(chunks):
    return [chunks[0]] + [ring(chunks[step], "y", step) for step in (1, 2, 3)]


def scatter_y(own, arrived, y):
    return send_along_y(chunks_for_y(own, arrived, y))


def scatter_zh(parts):
    total = add_up(parts).astype(BF16)
    return total, ring(total, "zh", 1)


def both_halves(pair):
    return add_up(pair).astype(BF16)


def rows_to_core(partial, core):
    partial = partial.astype(BF16).reshape(4, 2, TOK, D)

    def of_core(at):
        return lax.dynamic_index_in_dim(partial, at, 1, keepdims=False)

    return of_core(core), ring(of_core(1 - core), "core", 1)


def rows_along_x(total, x):
    def chunk(step):
        return lax.dynamic_index_in_dim(total, (x + step) % 4, 0, keepdims=False)

    far = ring(chunk(2).astype(BF16), "x", 2)
    ahead = ring(chunk(1).astype(BF16), "x", 1)
    behind = ring(chunk(3).astype(BF16), "x", -1)
    return chunk(0), ahead, behind, far


def exchange_x(blocks, x):
    def chunk(step):
        return lax.dynamic_index_in_dim(blocks, (x + step) % 4, 0, keepdims=False)

    return [chunk(0)] + [ring(chunk(step), "x", step) for step in (1, 2, 3)]


def put_exchanged(parts, others, x, core):
    rows = parts[0].shape[1]
    pieces = [*parts, others]
    copies, places = [], []
    for r in range(4):
        at = (x - r) % 4 * 2
        for tokens in range(2):
            copies += [(r, tokens, 1), (4, 2 * r + tokens, 1)]
            places += [tokens * GROUP + at + core, tokens * GROUP + at + 1 - core]
    places = jnp.stack(places).astype(jnp.int32)
    return put_in_place(places, pieces, copies, 2 * GROUP).reshape(2, GROUP, rows, TOK)


def far_rows_along_x(total, x):
    block = lax.dynamic_index_in_dim(total, (x + 2) % 4, 0, keepdims=False).astype(BF16)
    half = block.shape[0] // 2
    return ring(block[:half], "x", 1), ring(block[half:], "x", -1)


def near_rows_along_x(total, first, x):
    def chunk(step):
        return lax.dynamic_index_in_dim(total, (x + step) % 4, 0, keepdims=False)

    ahead, behind = chunk(1), chunk(3)
    half = ahead.shape[0] // 2
    ahead = jnp.concatenate([ahead[:half] + first[0].astype(F32), ahead[half:]])
    behind = jnp.concatenate([behind[:half], behind[half:] + first[1].astype(F32)])
    return chunk(0), ring(ahead.astype(BF16), "x", 1), ring(behind.astype(BF16), "x", -1)


def add_up(parts):
    return sum(part.astype(F32) for part in parts)


def rail_of(block):
    return [block, ring(block, "x", -1), ring(block, "x", 2), ring(block, "x", 1)]


def with_other_core(rail):
    return rail + [ring(part, "core", 1) for part in rail]


def swap_roles(values):
    return lax.ppermute(
        values,
        ("zl", "y", "x", "core"),
        [(a * GROUP + b, b * GROUP + a) for a in range(GROUP) for b in range(GROUP)],
    )


def after(values, *others):
    return lax.optimization_barrier((values, *others))[0]


def join(*groups):
    return lax.optimization_barrier(groups)


def heads_side_by_side(block):
    return jnp.concatenate(
        [block[i * HEAD_DIM : (i + 1) * HEAD_DIM] for i in range(HEADS_OWN)], axis=1
    )


def heads_stacked(block):
    return jnp.concatenate(
        [block[:, i * TOK : (i + 1) * TOK] for i in range(HEADS_OWN)], axis=0
    )


def allowed_keys(meta, j, start):
    half_at, head_end = meta[0], meta[1]
    shape = (KEY_CHUNK, ROWS_Q)
    column = lax.broadcasted_iota(jnp.int32, (1, ROWS_Q), 1)
    query = half_at * HALF + j * TOK + (column & (TOK - 1))
    first = jnp.where(
        query < head_end,
        0,
        jnp.where(query < head_end + MIDDLE, head_end, head_end + MIDDLE),
    )
    key = lax.broadcasted_iota(jnp.int32, shape, 0) + start + (half_at - 1) * HALF
    return (key <= query) & (key >= first)


def mask_scores(scores, meta, j, start, masked):
    parts = []
    for i in range(scores.shape[0] // KEY_CHUNK):
        part = scores[i * KEY_CHUNK : (i + 1) * KEY_CHUNK]
        if i in masked:
            part = jnp.where(allowed_keys(meta, j, start + i * KEY_CHUNK), part, NEG_LARGE)
        parts.append(part)
    return jnp.concatenate(parts) if len(parts) > 1 else parts[0]


def for_visible_keys(meta, j, step):
    chunks = HALF // KEY_CHUNK
    final = j == GROUP - 1

    @pl.when((meta[0] == 1) & jnp.logical_not(final))
    def _():
        step(0, HALF, (0,))

    @pl.when((meta[0] == 1) & final)
    def _():
        step(0, HALF, tuple(range(chunks)))

    for last in range(chunks):

        @pl.when((j * TOK // KEY_CHUNK == last) & jnp.logical_not(final))
        def _(last=last):
            step(HALF, (last + 1) * KEY_CHUNK, (0, last))

    @pl.when(final)
    def _():
        step(HALF, HALF, tuple(range(chunks)))


def dot_kn(left, right):
    return jnp.dot(left, right, preferred_element_type=F32)


def dot_nt(left, right):
    return lax.dot_general(
        left, right, (((1,), (1,)), ((), ())), preferred_element_type=F32
    )


def forward_kernel(
    meta, q_ref, kt_ref, vt_ref, out_ref, mixed_ref, lse_ref, k_ref, v_ref, top_ref, acc_ref
):
    j = pl.program_id(0)

    @pl.when(j == 0)
    def _():
        k_ref[...] = kt_ref[...].astype(F32).T.astype(BF16)
        row = lax.broadcasted_iota(jnp.int32, (V_ROWS - HEAD_DIM, 2 * HALF), 0)
        v_ref[:HEAD_DIM, :] = vt_ref[...]
        v_ref[HEAD_DIM:, :] = jnp.where(row == 0, 1.0, 0.0).astype(BF16)

    query = heads_side_by_side(q_ref[...])
    top_ref[...] = jnp.full_like(top_ref, NEG_LARGE)
    acc_ref[...] = jnp.zeros_like(acc_ref)

    def step(start, size, masked):
        rows = slice(start, start + size)
        scores = mask_scores(dot_kn(k_ref[rows, :], query), meta, j, start, masked)
        old = top_ref[...]
        new = jnp.maximum(old, jnp.max(scores, axis=0, keepdims=True))
        weights = jnp.exp(scores - new).astype(BF16)
        acc_ref[...] = acc_ref[...] * jnp.exp(old - new) + dot_kn(v_ref[:, rows], weights)
        top_ref[...] = new

    for_visible_keys(meta, j, step)
    total = acc_ref[HEAD_DIM : HEAD_DIM + 1, :]
    attended = heads_stacked(acc_ref[:HEAD_DIM, :] / total)
    out_ref[0] = attended
    mixed_ref[0] = attended.astype(BF16)
    lse_ref[...] = jnp.broadcast_to(top_ref[...] + jnp.log(total), lse_ref.shape)


def minus_rows(values):
    rows, rest = [], -values
    for _ in range(3):
        rows.append(rest.astype(BF16).astype(F32))
        rest = rest - rows[-1]
    zeros = jnp.zeros((EXTRA - 3, values.shape[1]), F32)
    return jnp.concatenate([*rows, zeros]).astype(BF16)


def backward_kernel(
    meta,
    q_ref,
    g_ref,
    o_ref,
    lse_ref,
    kt_ref,
    vt_ref,
    *rest,
    begin,
):
    dq_ref, dk_ref, dv_ref, k_ref, v_ref, acc_ref = rest[-6:]
    j = pl.program_id(0) + begin

    @pl.when(pl.program_id(0) == 0)
    def _():
        row = lax.broadcasted_iota(jnp.int32, (EXTRA, 2 * HALF), 0)
        ones = jnp.where(row < 3, 1.0, 0.0)
        k_ref[...] = jnp.concatenate([kt_ref[...].astype(F32), ones]).T.astype(BF16)
        v_ref[...] = jnp.concatenate([vt_ref[...].astype(F32), ones]).T.astype(BF16)
        if begin:
            dk_ref[...] = rest[0][...]
            dv_ref[...] = rest[1][...]
        else:
            dk_ref[...] = jnp.zeros_like(dk_ref)
            dv_ref[...] = jnp.zeros_like(dv_ref)

    query = heads_side_by_side(q_ref[...])
    grad = heads_side_by_side(g_ref[0])
    mixed = heads_side_by_side(o_ref[0])
    delta = jnp.sum(grad.astype(F32) * mixed, axis=0, keepdims=True)
    query_less = jnp.concatenate([query, minus_rows(lse_ref[0:1, :])])
    grad_less = jnp.concatenate([grad, minus_rows(delta)])
    acc_ref[...] = jnp.zeros_like(acc_ref)

    def step(start, size, masked):
        rows = slice(start, start + size)
        scores = mask_scores(dot_kn(k_ref[rows, :], query_less), meta, j, start, masked)
        probs = jnp.exp(scores)
        grad_scores = (probs * dot_kn(v_ref[rows, :], grad_less)).astype(BF16)
        acc_ref[...] += dot_kn(kt_ref[:, rows], grad_scores)
        dk_ref[:, rows] += dot_nt(query, grad_scores)
        dv_ref[:, rows] += dot_nt(grad, probs.astype(BF16))

    for_visible_keys(meta, j, step)
    dq_ref[0] = heads_stacked(acc_ref[...] * (1.0 / math.sqrt(HEAD_DIM)))


def whole(shape):
    return pl.BlockSpec(shape, lambda j, meta: (0,) * len(shape))


def token_block(rows):
    return pl.BlockSpec((rows, TOK), lambda j, meta: (0, j))


V_ROWS = 80
EXTRA = 16
LSE_ROWS = 8


def attend(meta, query_t, keys_t, values_t):
    return pl.pallas_call(
        forward_kernel,
        grid_spec=pltpu.PrefetchScalarGridSpec(
            num_scalar_prefetch=1,
            grid=(GROUP,),
            in_specs=[
                token_block(Q_OWN),
                whole((HEAD_DIM, 2 * HALF)),
                whole((HEAD_DIM, 2 * HALF)),
            ],
            out_specs=[
                pl.BlockSpec((1, Q_OWN, TOK), lambda j, meta: (j, 0, 0)),
                pl.BlockSpec((1, Q_OWN, TOK), lambda j, meta: (j, 0, 0)),
                pl.BlockSpec((LSE_ROWS, ROWS_Q), lambda j, meta: (j, 0)),
            ],
            scratch_shapes=[
                pltpu.VMEM((2 * HALF, HEAD_DIM), BF16),
                pltpu.VMEM((V_ROWS, 2 * HALF), BF16),
                pltpu.VMEM((1, ROWS_Q), F32),
                pltpu.VMEM((V_ROWS, ROWS_Q), F32),
            ],
        ),
        out_shape=[
            jax.ShapeDtypeStruct((GROUP, Q_OWN, TOK), F32),
            jax.ShapeDtypeStruct((GROUP, Q_OWN, TOK), BF16),
            jax.ShapeDtypeStruct((GROUP * LSE_ROWS, ROWS_Q), F32),
        ],
        compiler_params=pltpu.CompilerParams(vmem_limit_bytes=32 * 1024 * 1024),
        cost_estimate=cost(1),
        name="attend",
    )(meta, query_t, keys_t, values_t)


def attend_back(meta, begin, end, query_t, grad_t, attn_t, lse, keys_t, values_t, *sums):
    block = pl.BlockSpec((1, Q_OWN, TOK), lambda j, meta: (j + begin, 0, 0))
    return pl.pallas_call(
        functools.partial(backward_kernel, begin=begin),
        grid_spec=pltpu.PrefetchScalarGridSpec(
            num_scalar_prefetch=1,
            grid=(end - begin,),
            in_specs=[
                pl.BlockSpec((Q_OWN, TOK), lambda j, meta: (0, j + begin)),
                block,
                block,
                pl.BlockSpec((LSE_ROWS, ROWS_Q), lambda j, meta: (j + begin, 0)),
            ]
            + [whole((HEAD_DIM, 2 * HALF))] * (2 + len(sums)),
            out_specs=[
                pl.BlockSpec((1, Q_OWN, TOK), lambda j, meta: (j, 0, 0)),
                whole((HEAD_DIM, 2 * HALF)),
                whole((HEAD_DIM, 2 * HALF)),
            ],
            scratch_shapes=[
                pltpu.VMEM((2 * HALF, HEAD_DIM + EXTRA), BF16),
                pltpu.VMEM((2 * HALF, HEAD_DIM + EXTRA), BF16),
                pltpu.VMEM((HEAD_DIM, ROWS_Q), F32),
            ],
        ),
        out_shape=[
            jax.ShapeDtypeStruct((end - begin, Q_OWN, TOK), F32),
            jax.ShapeDtypeStruct((HEAD_DIM, 2 * HALF), F32),
            jax.ShapeDtypeStruct((HEAD_DIM, 2 * HALF), F32),
        ],
        compiler_params=pltpu.CompilerParams(vmem_limit_bytes=32 * 1024 * 1024),
        cost_estimate=cost(1),
        name="attend_back",
    )(meta, query_t, grad_t, attn_t, lse, keys_t, values_t, *sums)


def norm_kernel(places, *refs):
    (own, ahead, behind, low, high, own_two, near_two, far_two, weights) = refs[:9]
    normed_out, gains_out, gains = refs[9:]
    i = pl.program_id(0)

    @pl.when(i == 0)
    def _():
        gains[...] = weights[...].astype(F32).T[HEAD_DIM : HEAD_DIM + 8, :]
        gains_out[...] = gains[...]

    def norm(block, start, size, to):
        values = block[start : start + size, :].astype(F32)
        scale = lax.rsqrt(jnp.mean(values * values, axis=-1, keepdims=True) + EPSILON)
        normed_out[to : to + size, :] = (values * scale * gains[0:1, :]).astype(BF16)

    sources = [
        [(own, 0)],
        [(ahead, 0)],
        [(low, 0), (high, 0)],
        [(behind, 0)],
        [(own_two, 0)],
        [(near_two, 0)],
        [(far_two, 0)],
        [(near_two, TOK)],
    ]
    for at, parts in enumerate(sources):

        @pl.when(i == at)
        def _(parts=parts):
            size = TOK // len(parts)
            for k, (block, start) in enumerate(parts):
                norm(block, start, size, k * size)


def gather_norm(places, pieces, early_all):
    rows = [pl.BlockSpec(piece.shape, lambda i, places: (0, 0)) for piece in pieces]
    placed = pl.BlockSpec((TOK, D), lambda i, places: (places[i], 0))
    return pl.pallas_call(
        norm_kernel,
        grid_spec=pltpu.PrefetchScalarGridSpec(
            num_scalar_prefetch=1,
            grid=(GROUP,),
            in_specs=rows + [pl.BlockSpec((D, 128), lambda i, places: (0, 2))],
            out_specs=[
                placed,
                pl.BlockSpec((8, D), lambda i, places: (0, 0)),
            ],
            scratch_shapes=[pltpu.VMEM((8, D), F32)],
        ),
        out_shape=[
            jax.ShapeDtypeStruct((HALF, D), BF16),
            jax.ShapeDtypeStruct((8, D), F32),
        ],
        compiler_params=pltpu.CompilerParams(vmem_limit_bytes=32 * 1024 * 1024),
        cost_estimate=cost(1),
        name="gather_norm",
    )(places, *pieces, early_all)


def take_kernel(own, gate, up, out):
    for at in range(GROUP):

        @pl.when(own[0] == at)
        def _():
            parts = []
            for ref in (gate, up):
                for block in range(GROUP):
                    start = block * FF_OWN + at * SUB
                    low = start // 128 * 128
                    window = ref[:, low : low + 256].astype(F32)
                    parts.append(window[:, start - low : start - low + SUB])
            out[...] = jnp.concatenate(parts, axis=1).astype(BF16)


def take_columns(own, gate, up):
    rows = 64
    return pl.pallas_call(
        take_kernel,
        grid_spec=pltpu.PrefetchScalarGridSpec(
            num_scalar_prefetch=1,
            grid=(CHUNK // rows,),
            in_specs=[pl.BlockSpec((rows, FF), lambda i, own: (i, 0))] * 2,
            out_specs=pl.BlockSpec((rows, 2 * FF_OWN), lambda i, own: (i, 0)),
        ),
        out_shape=jax.ShapeDtypeStruct((CHUNK, 2 * FF_OWN), BF16),
        compiler_params=pltpu.CompilerParams(vmem_limit_bytes=32 * 1024 * 1024),
        cost_estimate=cost(1),
        name="take_columns",
    )(own, gate, up)


def gate_up_kernel(pieces, w_gate, w_up, gate, up, products):
    total = 0.0
    for which, (weight, out) in enumerate(((w_gate, gate), (w_up, up))):
        parts = []
        for block in range(GROUP):
            start = which * FF_OWN + block * SUB
            low = start // 128 * 128
            size = min(256, 2 * FF_OWN - low)
            for at in range(GROUP):
                window = pieces[at, :, low : low + size].astype(F32)
                parts.append(window[:, start - low : start - low + SUB])
        values = jnp.concatenate(parts, axis=1)
        out[...] = values
        total = total + jnp.sum(values * weight[...].astype(F32), axis=1, keepdims=True)
    products[...] = jnp.broadcast_to(total, products.shape)


def put_gate_up(pieces, w_gate, w_up):
    rows = 64
    row_block = pl.BlockSpec((rows, FF), lambda i: (i, 0))
    return pl.pallas_call(
        gate_up_kernel,
        grid=(CHUNK // rows,),
        in_specs=[
            pl.BlockSpec((GROUP, rows, 2 * FF_OWN), lambda i: (0, i, 0)),
            row_block,
            row_block,
        ],
        out_specs=[row_block, row_block, pl.BlockSpec((rows, 128), lambda i: (i, 0))],
        out_shape=[
            jax.ShapeDtypeStruct((CHUNK, FF), F32),
            jax.ShapeDtypeStruct((CHUNK, FF), F32),
            jax.ShapeDtypeStruct((CHUNK, 128), F32),
        ],
        compiler_params=pltpu.CompilerParams(vmem_limit_bytes=48 * 1024 * 1024),
        cost_estimate=cost(1),
        name="gate_up",
    )(pieces.reshape(GROUP, CHUNK, 2 * FF_OWN), w_gate, w_up)


def down_out_kernel(rows, down, out):
    values = rows[...].astype(F32)
    down[...] = values[:SUB]
    out[...] = values[SUB:]


def split_down_out(rows):
    return pl.pallas_call(
        down_out_kernel,
        grid=(GROUP,),
        in_specs=[pl.BlockSpec((SUB + OUT_SUB, D), lambda i: (i, 0))],
        out_specs=[
            pl.BlockSpec((SUB, D), lambda i: (i, 0)),
            pl.BlockSpec((OUT_SUB, D), lambda i: (i, 0)),
        ],
        out_shape=[
            jax.ShapeDtypeStruct((FF_OWN, D), F32),
            jax.ShapeDtypeStruct((Q_OWN, D), F32),
        ],
        compiler_params=pltpu.CompilerParams(vmem_limit_bytes=32 * 1024 * 1024),
        cost_estimate=cost(1),
        name="down_out",
    )(rows)


def qkv_kernel(places, *refs):
    pieces, weights, outs, products, stack = refs[:8], refs[8:11], refs[11:14], *refs[14:]
    query, key, value = outs
    for i, piece in enumerate(pieces):
        stack[places[i]] = piece[...]
    for at in range(GROUP):
        values = stack[at].astype(F32)
        query[:, at * Q_OWN : (at + 1) * Q_OWN] = values[:, :Q_OWN]
        head = key if at % 2 == 0 else value
        place = (at // 2) * HEAD_DIM
        head[:, place : place + HEAD_DIM] = values[:, Q_OWN : Q_OWN + HEAD_DIM]
    total = sum(
        jnp.sum(out[...] * weight[...].astype(F32), axis=1, keepdims=True)
        for out, weight in zip(outs, weights, strict=True)
    )
    products[...] = jnp.broadcast_to(total, (CHUNK, 128)).T[:8]


def assemble(kernel, places, pieces, rows, weights, shapes):
    count, width = pieces[0].shape
    return pl.pallas_call(
        kernel,
        grid_spec=pltpu.PrefetchScalarGridSpec(
            num_scalar_prefetch=1,
            grid=(count // rows,),
            in_specs=[pl.BlockSpec((rows, width), lambda i, places: (i, 0))] * 8
            + [pl.BlockSpec((rows, w.shape[1]), lambda i, places: (i, 0)) for w in weights],
            out_specs=[
                pl.BlockSpec((block, columns), lambda i, places: (i, 0))
                for _, block, columns in shapes
            ],
            scratch_shapes=[pltpu.VMEM((GROUP, rows, width), BF16)],
        ),
        out_shape=[jax.ShapeDtypeStruct((whole, columns), F32) for whole, _, columns in shapes],
        compiler_params=pltpu.CompilerParams(vmem_limit_bytes=48 * 1024 * 1024),
        cost_estimate=cost(1),
        name=kernel.__name__.removesuffix("_kernel"),
    )(places, *pieces, *weights)


def rms_scale(values):
    return lax.rsqrt(jnp.mean(values * values, axis=-1, keepdims=True) + EPSILON)


def rotate_t(values, cosine, sine_table):
    half = HEAD_DIM // 2
    first, second = values[:, :half], values[:, half:]
    return jnp.concatenate(
        [first * cosine - second * sine_table, second * cosine + first * sine_table], axis=1
    )


def norm_back(grad_normed, values, scale_rows, gain_full):
    unit_rows = values * scale_rows
    grad_unit = grad_normed * gain_full
    return scale_rows * (
        grad_unit - unit_rows * jnp.mean(grad_unit * unit_rows, axis=-1, keepdims=True)
    )


def contract(form, left, right):
    return jnp.einsum(form, left, right, preferred_element_type=F32)


def shards(
    inputs,
    positions,
    cotangent,
    w_query,
    w_key,
    w_value,
    w_out,
    w_gate,
    w_up,
    w_down,
    gain_attn,
    gain_mlp,
):
    zl, y, zh, x, core = (lax.axis_index(axis) for axis in AXES)
    xc = x * 2 + core
    group = ("x", "core")

    def gather_rows(rows):
        return lax.all_gather(rows, group, axis=0, tiled=True)

    inputs_near = near(inputs, "x")
    inputs_two = ring(inputs, "core", 1)

    index_here = (zh * GROUP + xc) * TOK + jnp.arange(TOK, dtype=jnp.int32)
    head_end = jnp.where(
        (zh == 0) & (xc == 0),
        jnp.sum((positions == index_here).astype(jnp.int32)),
        index_here[0] - positions[0],
    )
    meta = jnp.stack([zh, head_end]).astype(jnp.int32)
    rail = [((x + r) % 4) * 2 for r in range(4)]
    group_places = jnp.stack(
        [at + core for at in rail] + [at + 1 - core for at in rail]
    ).astype(jnp.int32)
    def columns(weight, width):
        return lax.dynamic_slice_in_dim(weight, xc * width, width, axis=1)

    kv_here = jnp.where(core == 0, w_key, w_value)
    kv_here = lax.dynamic_slice_in_dim(kv_here, x * HEAD_DIM, HEAD_DIM, axis=1)
    early = jnp.concatenate(
        [
            columns(w_query, Q_OWN),
            kv_here,
            gain_attn[:, None],
            gain_mlp[:, None],
            jnp.zeros((CHUNK, 62), BF16),
        ],
        axis=1,
    )
    early_near = near(early, "y")
    gate_up_here = take_columns(xc[None].astype(jnp.int32), w_gate, w_up)
    half_width = D // 2
    out_here = lax.dynamic_slice_in_dim(w_out, core * half_width, half_width, axis=1)
    down_here = stack_halves(lax.dynamic_slice_in_dim(w_down, xc * SUB, SUB, axis=0))
    early_blocks = (early, *early_near, *far(*early_near, "y"))
    early_blocks, inputs_near, out_here = join(early_blocks, inputs_near, out_here)
    early_z = across_z(*early_blocks)
    inputs_far = far(*inputs_near, "x")
    out_near = near(out_here, "y")
    early_z, inputs_far, inputs_two, gate_up_here = join(
        early_z, inputs_far, inputs_two, gate_up_here
    )
    inputs_rest = (
        ring(jnp.concatenate(inputs_near), "core", 1),
        ring(jnp.concatenate(inputs_far), "core", 1),
    )
    full_qkv_gains = put_weights(early_blocks, early_z, zl, y)
    full_qkv_gains, inputs_rest, out_near = join(full_qkv_gains, inputs_rest, out_near)
    out_far = far(*out_near, "y")
    gate_up_other = both_parities(gate_up_here)
    normed, gains = gather_norm(
        group_places,
        [inputs, *inputs_near, *inputs_far, inputs_two, *inputs_rest],
        full_qkv_gains,
    )
    full_qkv = full_qkv_gains[:, : Q_OWN + HEAD_DIM]
    full_gain_attn, full_gain_mlp = gains[0], gains[1]

    index_all = zh * HALF + jnp.arange(HALF, dtype=jnp.int32)
    doc_start = jnp.where(
        index_all < head_end,
        0,
        jnp.where(index_all < head_end + MIDDLE, head_end, head_end + MIDDLE),
    )
    frequency = THETA ** (-(jnp.arange(HEAD_DIM // 2, dtype=F32) * 2.0 / HEAD_DIM))
    angles = frequency[:, None] * (index_all - doc_start).astype(F32)[None, :]
    cosine, sine_table = jnp.cos(angles), jnp.sin(angles)
    is_key = core == 0
    cosine_kv = jnp.where(is_key, cosine, 1.0)
    sine_kv = jnp.where(is_key, sine_table, 0.0)

    raw_t = contract("dn,td->nt", full_qkv, normed)
    query_t = (
        rotate_t(raw_t[:Q_OWN].reshape(HEADS_OWN, HEAD_DIM, HALF), cosine, sine_table)
        .reshape(Q_OWN, HALF)
        .astype(BF16)
        * (1.0 / math.sqrt(HEAD_DIM))
    ).astype(BF16)
    kv_t = rotate_t(raw_t[Q_OWN:][None], cosine_kv, sine_kv)[0].astype(BF16)
    kv_other = ring(kv_t, "core", 1)
    kv_prev = lax.ppermute(kv_t, "zh", [(0, 1)])
    kv_prev_other = lax.ppermute(kv_t, ("zh", "core"), [(0, 3), (1, 2)])
    kv_t, kv_other, kv_prev, kv_prev_other, query_t, gate_up_here, gate_up_other, out_far = join(
        kv_t, kv_other, kv_prev, kv_prev_other, query_t, gate_up_here, gate_up_other, out_far
    )
    mine = jnp.concatenate([kv_prev, kv_t], axis=1)
    theirs = jnp.concatenate([kv_prev_other, kv_other], axis=1)
    keys_t = jnp.where(is_key, mine, theirs)
    values_t = jnp.where(is_key, theirs, mine)
    out_blocks = (out_here, *out_near, *out_far)
    out_z = across_z(*out_blocks)
    gate_up_pair = jnp.concatenate([gate_up_here, *gate_up_other])
    gate_up_near = near(gate_up_pair, "y")
    attended = attend(meta, query_t, keys_t, values_t)
    (attn_t, mixed_t, lse), out_z, gate_up_near = join(attended, out_z, gate_up_near)
    mixed_parts = exchange_x(mixed_t.reshape(4, 2, Q_OWN, TOK), x)
    gate_up_far = far(*gate_up_near, "y")
    out_half = put_weights(out_blocks, out_z, zl, y)
    mixed_parts, out_half = join(mixed_parts, out_half)
    mixed_others = ring(jnp.concatenate(mixed_parts), "core", 1)
    mixed_others, mixed_parts = join(mixed_others, mixed_parts)
    mixed_both = put_exchanged(mixed_parts, mixed_others, x, core)

    def of_core(values, at):
        return lax.dynamic_index_in_dim(values, at, 0, keepdims=False)

    out_rows = contract("ckt,kd->ctd", mixed_both.reshape(2, D, TOK), out_half).astype(BF16)
    out_mine = of_core(out_rows, core)
    out_theirs = ring(of_core(out_rows, 1 - core), "core", 1)
    out_theirs, down_here, cotangent_here = join(out_theirs, down_here, cotangent)
    tokens_here = inputs.astype(F32)
    residual = tokens_here + jnp.concatenate(
        [
            jnp.where(core == 0, out_mine, out_theirs),
            jnp.where(core == 0, out_theirs, out_mine),
        ],
        axis=1,
    ).astype(F32)
    scale_mlp = rms_scale(residual)
    normed_rows = (residual * scale_mlp * full_gain_mlp).astype(BF16)
    normed_mlp = gather_rows(normed_rows)
    down_other = both_parities(down_here)
    cotangent_near = near(cotangent_here, "x")
    down_other, cotangent_near, gate_up_far = join(down_other, cotangent_near, gate_up_far)
    down_pair = jnp.concatenate([down_here, *down_other])
    down_near = near(down_pair, "y")
    cotangent_far = far(*cotangent_near, "x")
    gate_up_all = put_pairs(gate_up_pair, gate_up_near, gate_up_far, zl, y)
    normed_mlp, gate_up_all, down_near, cotangent_far = join(
        normed_mlp, gate_up_all, down_near, cotangent_far
    )

    gate_up = contract("td,df->tf", normed_mlp, gate_up_all)
    down_far = far(*down_near, "y")
    cotangent_blocks = (cotangent_here, *cotangent_near, *cotangent_far)
    cotangent_two = swap_blocks(*cotangent_blocks)
    gate_up, down_far, cotangent_two = join(gate_up, down_far, cotangent_two)
    cotangent_all = put_rows(cotangent_blocks, cotangent_two, group_places)
    full_down = put_row_pairs(down_pair, down_near, down_far, zl, y)
    grad_hidden = contract("td,fd->tf", cotangent_all, full_down)
    gate, upward = gate_up[:, :FF_OWN], gate_up[:, FF_OWN:]
    sigmoid_gate = jax.nn.sigmoid(gate)
    silu_gate = gate * sigmoid_gate
    hidden = (silu_gate * upward).astype(BF16)
    grad_acts = jnp.concatenate(
        [
            (grad_hidden * upward * sigmoid_gate * (1.0 + gate * (1.0 - sigmoid_gate))).astype(BF16),
            (grad_hidden * silu_gate).astype(BF16),
        ],
        axis=1,
    )
    back_rows = rows_to_core(contract("tf,df->td", grad_acts, gate_up_all), core)

    def columns_at(values, start, count):
        return lax.dynamic_slice_in_dim(values, start * CHUNK, count * CHUNK, axis=1)

    other = (1 - zl) * 4

    def gate_up_product(start, count):
        rows = contract("td,tf->df", columns_at(normed_mlp, start, count), grad_acts)
        return rows.astype(BF16).reshape(count, CHUNK, 2 * FF_OWN)

    gate_up_theirs = gate_up_product(other, 4)
    back_total = back_rows[0].astype(F32) + back_rows[1].astype(F32)
    back_total, gate_up_pairs, hidden, normed_mlp, grad_acts = join(
        back_total, (gate_up_theirs[:2], gate_up_theirs[2:]), hidden, normed_mlp, grad_acts
    )
    back_rows = rows_along_x(back_total, x)
    gate_up_z = scatter_z(gate_up_pairs)
    gate_up_mine = gate_up_product(zl * 4, 4)
    part_down = contract("tf,td->fd", hidden, cotangent_all).astype(BF16)
    part_down = part_down.reshape(8, SUB, D)
    part_output = contract("tf,fd->td", hidden, full_down).astype(BF16)
    back_rows, gate_up_z, gate_up_mine, part_down, part_output = join(
        back_rows, gate_up_z, gate_up_mine, part_down, part_output
    )
    gate_up_far = far_along_y(gate_up_mine, gate_up_z, y)
    grad_normed_mlp = add_up(back_rows)
    grad_residual = cotangent.astype(F32) + norm_back(
        grad_normed_mlp, residual, scale_mlp, full_gain_mlp
    )
    grad_here = grad_residual.astype(BF16)
    grad_theirs = ring(grad_here, "core", 1)
    grad_theirs, grad_here = join(grad_theirs, grad_here)
    grad_both = jnp.stack(
        [jnp.where(core == 0, grad_here, grad_theirs), jnp.where(core == 0, grad_theirs, grad_here)]
    )
    grad_both = jnp.where(core == 0, grad_both[..., :half_width], grad_both[..., half_width:])
    grad_partial = contract("kd,ctd->kct", out_half, grad_both).reshape(4, 2, Q_OWN, 2, TOK)

    def heads_of(at):
        return lax.dynamic_index_in_dim(grad_partial, at, 1, keepdims=False)

    grad_arrived = ring(heads_of(1 - core).astype(BF16), "core", 1)
    grad_arrived, gate_up_far = join(grad_arrived, gate_up_far)
    grad_heads = (heads_of(core) + grad_arrived.astype(F32)).astype(BF16)
    grad_parts = exchange_x(grad_heads.transpose(0, 2, 1, 3), x)
    grad_attn_out = gather_rows(grad_here)
    gate_up_y = near_along_y(gate_up_mine, gate_up_z, gate_up_far, y)
    grad_parts, gate_up_y, part_output = join(grad_parts, gate_up_y, part_output)
    output_rows = lax.psum_scatter(part_output, group, scatter_dimension=0, tiled=True)
    gate_up_zh = scatter_zh(gate_up_y)
    places = jnp.stack([(x - r) % 4 * 2 for r in range(4)]).astype(jnp.int32)
    grad_mixed_t = put_in_place(places, grad_parts, [(r, 0, 2) for r in range(4)], GROUP)
    back_args = (query_t, grad_mixed_t, attn_t, lse, keys_t, values_t)
    attended = attend_back(meta, 0, 4, *back_args)
    (query_0, *key_sums), gate_up_zh, grad_attn_out = join(attended, gate_up_zh, grad_attn_out)
    shard_gate_up = both_halves(gate_up_zh)
    part_out = contract(
        "bkt,btd->kd", mixed_t, grad_attn_out.reshape(GROUP, TOK, D)
    ).astype(BF16)
    part_down_out = jnp.concatenate([part_down, part_out.reshape(8, OUT_SUB, D)], axis=1)

    def chunks(start, count):
        return lax.dynamic_slice_in_dim(part_down_out, start, count, axis=0)

    down_out_pairs = (chunks(other, 2), chunks(other + 2, 2))
    down_out_pairs, key_sums = join(down_out_pairs, key_sums)
    down_out_z = scatter_z(down_out_pairs)
    attended = attend_back(meta, 4, 8, *back_args, *key_sums)
    (query_1, grad_keys_t, grad_values_t), down_out_z, output_rows, shard_gate_up = join(
        attended, down_out_z, output_rows, shard_gate_up
    )
    gate_up_grads = gather_rows(shard_gate_up)
    grad_query_t = jnp.concatenate([query_0, query_1])

    kept = jnp.where(is_key, grad_keys_t, grad_values_t)
    given = jnp.where(is_key, grad_values_t, grad_keys_t)
    arrived = ring(given.astype(BF16), "core", 1)
    arrived, kept, grad_query_t = join(arrived, kept, grad_query_t)
    grad_kv = kept + arrived.astype(F32)
    from_next = lax.ppermute(grad_kv[:, :HALF].astype(BF16), "zh", [(1, 0)])
    from_next, grad_kv, grad_query_t = join(from_next, grad_kv, grad_query_t)
    down_out_y = scatter_y(chunks(zl * 4, 4), down_out_z, y)
    grad_kv_t = grad_kv[:, HALF:] + from_next.astype(F32)

    def by_block(table):
        return table.reshape(-1, GROUP, TOK).transpose(1, 0, 2)

    half_head = HEAD_DIM // 2
    cosine_b, sine_b = by_block(cosine)[:, None], by_block(sine_table)[:, None]
    first = grad_query_t.reshape(GROUP, HEADS_OWN, HEAD_DIM, TOK)[:, :, :half_head]
    second = grad_query_t.reshape(GROUP, HEADS_OWN, HEAD_DIM, TOK)[:, :, half_head:]
    turned = jnp.concatenate(
        [first * cosine_b + second * sine_b, second * cosine_b - first * sine_b], axis=2
    ).reshape(GROUP, Q_OWN, TOK)
    grad_qkv = jnp.concatenate(
        [turned, by_block(rotate_t(grad_kv_t[None], cosine_kv, -sine_kv)[0])], axis=1
    ).astype(BF16)
    grad_qkv_rows = grad_qkv.transpose(0, 2, 1).reshape(HALF, Q_OWN + HEAD_DIM)
    part_normed = contract("tn,dn->td", grad_qkv_rows, full_qkv).astype(BF16)

    def qkv_product(start, count):
        rows = contract("td,tn->dn", columns_at(normed, start, count), grad_qkv_rows)
        return rows.astype(BF16).reshape(count, CHUNK, Q_OWN + HEAD_DIM)

    qkv_pairs = [qkv_product(other, 2), qkv_product(other + 2, 2)]
    normed_pair = rows_to_core(part_normed, core)
    normed_pair, qkv_pairs, grad_qkv_rows = join(normed_pair, qkv_pairs, grad_qkv_rows)
    qkv_z = scatter_z(qkv_pairs)
    qkv_mine = qkv_product(zl * 4, 4)
    normed_total = normed_pair[0].astype(F32) + normed_pair[1].astype(F32)
    qkv_z, qkv_mine, down_out_y, normed_total = join(qkv_z, qkv_mine, down_out_y, normed_total)
    qkv_y = scatter_y(qkv_mine, qkv_z, y)
    normed_first = far_rows_along_x(normed_total, x)
    down_out_zh = scatter_zh(down_out_y)
    qkv_y, down_out_zh, normed_total, normed_first, gate_up_grads = join(
        qkv_y, down_out_zh, normed_total, normed_first, gate_up_grads
    )
    qkv_zh = scatter_zh(qkv_y)
    normed_parts = near_rows_along_x(normed_total, normed_first, x)
    shard_down_out = both_halves(down_out_zh)
    turned_out = swap_roles(shard_down_out[SUB:])
    qkv_zh, turned_out, normed_parts, gate_up_grads = join(
        qkv_zh, turned_out, normed_parts, gate_up_grads
    )
    grad_gate, grad_up, mlp_products = put_gate_up(gate_up_grads, w_gate, w_up)
    down_out_all = gather_rows(jnp.concatenate([shard_down_out[:SUB], turned_out]))
    qkv_rail = rail_of(both_halves(qkv_zh))
    grad_normed = add_up(normed_parts)
    output = (residual + output_rows.astype(F32)).astype(BF16)
    scale_here = rms_scale(tokens_here)
    grad_inputs = grad_residual + norm_back(grad_normed, tokens_here, scale_here, full_gain_attn)

    grad_down, grad_out = split_down_out(down_out_all)
    kv_columns = KV_HEADS * HEAD_DIM
    grad_query, grad_key, grad_value, attn_products = assemble(
        qkv_kernel,
        group_places,
        with_other_core(qkv_rail),
        CHUNK,
        [w_query, w_key, w_value],
        [
            (CHUNK, CHUNK, HEADS * HEAD_DIM),
            (CHUNK, CHUNK, kv_columns),
            (CHUNK, CHUNK, kv_columns),
            (8, 8, CHUNK),
        ],
    )
    return (
        output,
        grad_inputs,
        grad_query,
        grad_key,
        grad_value,
        grad_out,
        grad_gate,
        grad_up,
        grad_down,
        attn_products[0] / gain_attn.astype(F32),
        mlp_products[:, 0] / gain_mlp.astype(F32),
    )


def solution(mesh):
    split = Mesh(mesh.devices.reshape(2, 4, 2, 4, 2), AXES)
    dp, tokens = ("zl", "y"), AXES
    matrix = P(dp, None)
    return jax.shard_map(
        shards,
        mesh=split,
        in_specs=(
            P(tokens, None),
            P(tokens),
            P(tokens, None),
            matrix,
            matrix,
            matrix,
            matrix,
            matrix,
            matrix,
            matrix,
            P(dp),
            P(dp),
        ),
        out_specs=(
            P(tokens, None),
            P(tokens, None),
            matrix,
            matrix,
            matrix,
            matrix,
            matrix,
            matrix,
            matrix,
            P(dp),
            P(dp),
        ),
        check_vma=False,
    )
```

profile of v0, /device:TPU:1, one launch (start us, length us, event | category | flops | bytes accessed | tf_op | source)
XLA Modules:
  0.0 510.3 jit_solution(17758091104249753161)
XLA Ops:
  93.6 7.3 %attend.1 = (f32[8,256,128]{2,1,0:T(8,128)S(1)}, bf16[8,256,128]{2,1,0:T(8,128)(2,1)S(1)}, f32[64,512]{1,0:T(8,128)S(1)}) custom-call(s32[2]{0:T(128)S(1)} %pad_add_fusion.meta, bf16[256,1024]{1,0:T(8,128)(2,1)S(1)} %bitcast.305, bf16[64,2048]{1,0:T(8,128)(2,1)S(1)} %get-tuple-element.405.kt_ref, bf16[64,2048]{1,0:T(8,128)(2,1)S(1)} %get-tuple-element.404.vt_ref), custom_call_target="tpu_custom_call" | custom-call | flops 1000000000 | bytes 3000000 | tf_op jit(solution)/shard_map/attend/pallas_call | solution.py:513
  101.6 7.9 %collective-permute-done.22 = bf16[512,1024]{1,0:T(8,128)(2,1)} collective-permute-done((bf16[512,1024]{1,0:T(8,128)(2,1)}, bf16[512,1024]{1,0:T(8,128)(2,1)}, u32[]{:S(2)}, u32[]{:S(2)}) %collective-permute-start.22) | collective-permute-done | bytes 1048608 | tf_op jit(solution)/shard_map/ppermute | solution.py:43
  143.9 10.8 %collective-permute-done.35 = bf16[256,1408]{1,0:T(8,128)(2,1)S(1)} collective-permute-done((bf16[256,1408]{1,0:T(8,128)(2,1)S(1)}, bf16[256,1408]{1,0:T(8,128)(2,1)S(1)}, u32[]{:S(2)}, u32[]{:S(2)}) %collective-permute-start.35) | collective-permute-done | bytes 720928 | tf_op jit(solution)/shard_map/ppermute | solution.py:45
  177.1 4.7 put_in_place.9
  193.3 10.4 %fusion.98 = f32[1024,1408]{1,0:T(8,128)S(1)} fusion(bf16[1024,2048]{1,0:T(8,128)(2,1)} %all-gather.5.cloned.1.call-done, bf16[2048,1408]{1,0:T(8,128)(2,1)} %bitcast.291), kind=kOutput, calls=%fused_computation.261 | convolution fusion | flops 5905580032 | bytes 15728640 | tf_op jit(solution)/shard_map/td,df->tf/dot_general | solution.py:799
  209.7 5.5 %multiply_convert_fusion.2 = (bf16[1024,704]{1,0:T(8,128)(2,1)S(1)}, bf16[1024,704]{1,0:T(8,128)(2,1)S(1)}, bf16[1024,704]{1,0:T(8,128)(2,1)}) fusion(f32[1024,1408]{1,0:T(8,128)S(1)} %fusion.98, bf16[1024,2048]{1,0:T(8,128)(2,1)S(1)} %bitcast.296, bf16[704,2048]{1,0:T(8,128)(2,1)S(1)} %bitcast.303), kind=kOutput, calls=%fused_computation.26 | convolution fusion | flops 2963603456 | bytes 17170432 | tf_op jit(solution)/shard_map/td,fd->tf/dot_general | solution.py:799
  216.1 6.9 %convolution_convert_fusion.2 = bf16[1024,2048]{1,0:T(8,128)(2,1)S(1)} fusion(bf16[1024,1408]{1,0:T(8,128)(2,1)S(1)} %pad_maximum_fusion, bf16[2048,1408]{1,0:T(8,128)(2,1)S(1)} %bitcast.294), kind=kOutput, calls=%fused_computation.20 | convolution fusion | flops 5907677184 | bytes 12845056 | tf_op jit(solution)/shard_map/tf,df->td/dot_general | solution.py:799
  225.7 5.9 %convolution_convert_fusion.4 = bf16[1024,1408]{1,0:T(8,128)(2,1)S(1)} fusion(bf16[1024,1408]{1,0:T(8,128)(2,1)} %copy-done.86, bf16[1024,2048]{1,0:T(8,128)(2,1)} %all-gather.5.cloned.1.call-done, s32[]{:T(128)S(6)} %select_n.522), kind=kOutput, calls=%fused_computation.22 | convolution fusion | flops 2954231808 | bytes 7864324 | tf_op jit(solution)/shard_map/td,tf->df/dot_general | solution.py:799
  243.9 4.9 convolution_convert_fusion.1
  248.9 7.6 %convolution_convert_fusion.5 = bf16[704,2048]{1,0:T(8,128)(2,1)} fusion(bf16[1024,704]{1,0:T(8,128)(2,1)} %get-tuple-element.254, bf16[1024,2048]{1,0:T(8,128)(2,1)} %bitcast.297), kind=kOutput, calls=%fused_computation.23 | convolution fusion | flops 2954231808 | bytes 8519680 | tf_op jit(solution)/shard_map/tf,td->fd/dot_general | solution.py:799
  256.5 4.8 convolution_convert_fusion.3
  264.3 10.4 %collective-permute-done.50 = bf16[2,256,1408]{2,1,0:T(8,128)(2,1)S(1)} collective-permute-done((bf16[2,256,1408]{2,1,0:T(8,128)(2,1)}, bf16[2,256,1408]{2,1,0:T(8,128)(2,1)S(1)}, u32[]{:S(2)}, u32[]{:S(2)}) %collective-permute-start.50) | collective-permute-done | bytes 1441824 | tf_op jit(solution)/shard_map/ppermute | solution.py:43
  284.4 4.8 convert_add_fusion.3
  294.7 5.6 %collective-permute-done.54 = bf16[128,1408]{1,0:T(8,128)(2,1)S(1)} collective-permute-done((bf16[128,1408]{1,0:T(8,128)(2,1)S(1)}, bf16[128,1408]{1,0:T(8,128)(2,1)S(1)}, u32[]{:S(2)}, u32[]{:S(2)}) %collective-permute-start.54) | collective-permute-done | bytes 360480 | tf_op jit(solution)/shard_map/ppermute | solution.py:45
  312.8 5.8 %collective-permute-done.57.refs_2_ = bf16[2,256,128]{2,1,0:T(8,128)(2,1)S(1)} collective-permute-done((bf16[2,256,128]{2,1,0:T(8,128)(2,1)S(1)}, bf16[2,256,128]{2,1,0:T(8,128)(2,1)S(1)}, u32[]{:S(2)}, u32[]{:S(2)}) %collective-permute-start.57) | collective-permute-done | bytes 131104 | tf_op jit(solution)/shard_map/ppermute | solution.py:45
  324.7 4.5 attend_back.2
  331.6 7.5 %collective-permute-done.61 = bf16[256,1408]{1,0:T(8,128)(2,1)} collective-permute-done((bf16[256,1408]{1,0:T(8,128)(2,1)}, bf16[256,1408]{1,0:T(8,128)(2,1)}, u32[]{:S(2)}, u32[]{:S(2)}) %collective-permute-start.61) | collective-permute-done | bytes 720928 | tf_op jit(solution)/shard_map/ppermute | solution.py:45
  347.4 7.2 %attend_back.3 = (f32[4,256,128]{2,1,0:T(8,128)S(1)}, f32[64,2048]{1,0:T(8,128)S(1)}, f32[64,2048]{1,0:T(8,128)S(1)}) custom-call(s32[2]{0:T(128)S(1)} %pad_add_fusion.meta, bf16[256,1024]{1,0:T(8,128)(2,1)S(1)} %bitcast.307, bf16[8,256,128]{2,1,0:T(8,128)(2,1)S(1)} %copy-done.47, f32[8,256,128]{2,1,0:T(8,128)S(1)} %copy-done.31, f32[64,512]{1,0:T(8,128)S(1)} %copy-done.59, ...), custom_call_target="tpu_custom_call" | custom-call | flops 1000000000 | bytes 3000000 | tf_op jit(solution)/shard_map/attend_back/pallas_call | solution.py:548
  357.9 8.3 %collective-permute-done.62 = bf16[2,120,2048]{2,1,0:T(8,128)(2,1)} collective-permute-done((bf16[2,120,2048]{2,1,0:T(8,128)(2,1)}, bf16[2,120,2048]{2,1,0:T(8,128)(2,1)}, u32[]{:S(2)}, u32[]{:S(2)}) %collective-permute-start.62) | collective-permute-done | bytes 983072 | tf_op jit(solution)/shard_map/ppermute | solution.py:43
  373.5 6.3 %collective-permute-done.65 = bf16[64,1024]{1,0:T(8,128)(2,1)S(1)} collective-permute-done((bf16[64,1024]{1,0:T(8,128)(2,1)S(1)}, bf16[64,1024]{1,0:T(8,128)(2,1)S(1)}, u32[]{:S(2)}, u32[]{:S(2)}) %collective-permute-start.65) | collective-permute-done | bytes 131104 | tf_op jit(solution)/shard_map/ppermute | solution.py:1054
  446.7 4.7 collective-permute-start.79
  455.4 12.7 %collective-permute-start.82 = (bf16[256,320]{1,0:T(8,128)(2,1)S(1)}, bf16[256,320]{1,0:T(8,128)(2,1)S(1)}, u32[]{:S(2)}, u32[]{:S(2)}) collective-permute-start(bf16[256,320]{1,0:T(8,128)(2,1)S(1)} %add_convert_fusion.11.refs_0_), channel_id=1, source_target_pairs={{0,6},{2,0},{4,2},{6,4},{1,7},{3,1},{5,3},{7,5},{8,14},{10,8},{12,... | collective-permute-start | bytes 491528 | tf_op jit(solution)/shard_map/ppermute | solution.py:45
  473.8 9.2 %gate_up.1 = (f32[256,5632]{1,0:T(8,128)}, f32[256,5632]{1,0:T(8,128)}, f32[256,128]{1,0:T(8,128)S(1)}) custom-call(bf16[8,256,1408]{2,1,0:T(8,128)(2,1)} %bitcast.335, bf16[256,5632]{1,0:T(8,128)(2,1)S(1)} %copy-done.7, bf16[256,5632]{1,0:T(8,128)(2,1)S(1)} %copy-done.9), custom_call_target="tpu_custom_call" | custom-call | flops 1000000000 | bytes 3000000 | tf_op jit(solution)/shard_map/gate_up/pallas_call | solution.py:693
  488.7 8.6 %all-gather.11.cloned.1.call-done.rows = bf16[960,2048]{1,0:T(8,128)(2,1)} async-done(((bf16[120,2048]{1,0:T(8,128)(2,1)}), bf16[960,2048]{1,0:T(8,128)(2,1)}) %all-gather.11.cloned.1.call-update) | async-done | bytes 3932176 | tf_op jit(solution)/shard_map/all_gather | solution.py:821
  (562 shorter events, 320.2 us)
Async XLA Ops:
  7.2 178.9 %all-gather.5.cloned.1.call-start = ((), (), s32[]{:S(2)}) async-start(), calls=%async_computation.1 | async-start | bytes 4718592 | tf_op jit(solution)/shard_map/all_gather | solution.py:821
  47.0 23.9 %collective-permute-start.18 = (bf16[128,1408]{1,0:T(8,128)(2,1)S(1)}, bf16[128,1408]{1,0:T(8,128)(2,1)S(1)}, u32[]{:S(2)}, u32[]{:S(2)}) collective-permute-start(bf16[128,1408]{1,0:T(8,128)(2,1)S(1)} %get-tuple-element.391), channel_id=1, source_target_pairs={{0,64},{64,8},{8,72},{72,0},{1,65},{65,9},{9,73},{73,1},{2,66},{66... | collective-permute-start | bytes 1081352 | tf_op jit(solution)/shard_map/ppermute | solution.py:43
  82.9 31.9 %collective-permute-start.24 = (bf16[512,1408]{1,0:T(8,128)(2,1)}, bf16[512,1408]{1,0:T(8,128)(2,1)S(1)}, u32[]{:S(2)}, u32[]{:S(2)}) collective-permute-start(bf16[512,1408]{1,0:T(8,128)(2,1)} %constant_dynamic-update-slice_fusion.4), channel_id=1, source_target_pairs={{0,48},{16,0},{32,16},{48,32},{1,49},{17,1},{33,17},{49,33},{2,50}... | collective-permute-start | bytes 4325384 | tf_op jit(solution)/shard_map/ppermute | solution.py:45
  83.3 33.1 %collective-permute-start.25 = (bf16[512,1408]{1,0:T(8,128)(2,1)}, bf16[512,1408]{1,0:T(8,128)(2,1)}, u32[]{:S(2)}, u32[]{:S(2)}) collective-permute-start(bf16[512,1408]{1,0:T(8,128)(2,1)} %constant_dynamic-update-slice_fusion.4), channel_id=1, source_target_pairs={{0,16},{16,32},{32,48},{48,0},{1,17},{17,33},{33,49},{49,1},{2,18}... | collective-permute-start | bytes 4325384 | tf_op jit(solution)/shard_map/ppermute | solution.py:45
  85.4 24.1 %collective-permute-start.22 = (bf16[512,1024]{1,0:T(8,128)(2,1)}, bf16[512,1024]{1,0:T(8,128)(2,1)}, u32[]{:S(2)}, u32[]{:S(2)}) collective-permute-start(bf16[512,1024]{1,0:T(8,128)(2,1)} %pad_maximum_fusion.2), channel_id=1, source_target_pairs={{0,64},{64,8},{8,72},{72,0},{1,65},{65,9},{9,73},{73,1},{2,66},{66... | collective-permute-start | bytes 3145736 | tf_op jit(solution)/shard_map/ppermute | solution.py:43
  87.2 23.2 %collective-permute-start.23 = (bf16[512,1024]{1,0:T(8,128)(2,1)}, bf16[512,1024]{1,0:T(8,128)(2,1)}, u32[]{:S(2)}, u32[]{:S(2)}) collective-permute-start(bf16[512,1024]{1,0:T(8,128)(2,1)} %pad_maximum_fusion.3), channel_id=1, source_target_pairs={{0,72},{64,0},{8,64},{72,8},{1,73},{65,1},{9,65},{73,9},{2,74},{66... | collective-permute-start | bytes 3145736 | tf_op jit(solution)/shard_map/ppermute | solution.py:43
  137.2 201.9 %all-gather.7.cloned.1.call-start = ((), (), s32[]{:S(2)}) async-start(), calls=%async_computation.2 | async-start | bytes 4718592 | tf_op jit(solution)/shard_map/all_gather | solution.py:821
  140.1 22.0 %collective-permute-start.33 = (bf16[128,2048]{1,0:T(8,128)(2,1)}, bf16[128,2048]{1,0:T(8,128)(2,1)S(1)}, u32[]{:S(2)}, u32[]{:S(2)}) collective-permute-start(bf16[128,2048]{1,0:T(8,128)(2,1)} %param.14), channel_id=1, source_target_pairs={{0,6},{2,0},{4,2},{6,4},{1,7},{3,1},{5,3},{7,5},{8,14},{10,8},{12,... | collective-permute-start | bytes 1572872 | tf_op jit(solution)/shard_map/ppermute | solution.py:45
  142.0 24.4 %collective-permute-start.34 = (bf16[128,2048]{1,0:T(8,128)(2,1)}, bf16[128,2048]{1,0:T(8,128)(2,1)S(1)}, u32[]{:S(2)}, u32[]{:S(2)}) collective-permute-start(bf16[128,2048]{1,0:T(8,128)(2,1)} %param.14), channel_id=1, source_target_pairs={{0,2},{2,4},{4,6},{6,0},{1,3},{3,5},{5,7},{7,1},{8,10},{10,12},{12... | collective-permute-start | bytes 1572872 | tf_op jit(solution)/shard_map/ppermute | solution.py:45
  169.7 34.1 %collective-permute-start.43 = (bf16[128,2048]{1,0:T(8,128)(2,1)}, bf16[128,2048]{1,0:T(8,128)(2,1)}, u32[]{:S(2)}, u32[]{:S(2)}) collective-permute-start(bf16[128,2048]{1,0:T(8,128)(2,1)} %param.14), channel_id=1, source_target_pairs={{0,1},{1,0},{2,3},{3,2},{4,5},{5,4},{6,7},{7,6},{8,9},{9,8},{10,11... | collective-permute-start | bytes 1572872 | tf_op jit(solution)/shard_map/ppermute | solution.py:45
  238.6 25.8 %collective-permute-start.47 = (bf16[128,2048]{1,0:T(8,128)(2,1)}, bf16[128,2048]{1,0:T(8,128)(2,1)}, u32[]{:S(2)}, u32[]{:S(2)}) collective-permute-start(bf16[128,2048]{1,0:T(8,128)(2,1)} %get-tuple-element.369), channel_id=1, source_target_pairs={{0,2},{2,4},{4,6},{6,0},{1,3},{3,5},{5,7},{7,1},{8,10},{10,12},{12... | collective-permute-start | bytes 1572872 | tf_op jit(solution)/shard_map/ppermute | solution.py:45
  238.6 25.8 %collective-permute-start.48 = (bf16[128,2048]{1,0:T(8,128)(2,1)}, bf16[128,2048]{1,0:T(8,128)(2,1)}, u32[]{:S(2)}, u32[]{:S(2)}) collective-permute-start(bf16[128,2048]{1,0:T(8,128)(2,1)} %get-tuple-element.368), channel_id=1, source_target_pairs={{0,6},{2,0},{4,2},{6,4},{1,7},{3,1},{5,3},{7,5},{8,14},{10,8},{12,... | collective-permute-start | bytes 1572872 | tf_op jit(solution)/shard_map/ppermute | solution.py:45
  241.2 23.1 %collective-permute-start.49 = (bf16[128,2048]{1,0:T(8,128)(2,1)}, bf16[128,2048]{1,0:T(8,128)(2,1)}, u32[]{:S(2)}, u32[]{:S(2)}) collective-permute-start(bf16[128,2048]{1,0:T(8,128)(2,1)} %get-tuple-element.367), channel_id=1, source_target_pairs={{0,4},{2,6},{4,0},{6,2},{1,5},{3,7},{5,1},{7,3},{8,12},{10,14},{12... | collective-permute-start | bytes 1572872 | tf_op jit(solution)/shard_map/ppermute | solution.py:45
  241.2 33.5 %collective-permute-start.50 = (bf16[2,256,1408]{2,1,0:T(8,128)(2,1)}, bf16[2,256,1408]{2,1,0:T(8,128)(2,1)S(1)}, u32[]{:S(2)}, u32[]{:S(2)}) collective-permute-start(bf16[2,256,1408]{2,1,0:T(8,128)(2,1)} %bitcast.110), channel_id=1, source_target_pairs={{0,64},{64,8},{8,72},{72,0},{1,65},{65,9},{9,73},{73,1},{2,66},{66... | collective-permute-start | bytes 4325384 | tf_op jit(solution)/shard_map/ppermute | solution.py:43
  241.2 33.5 %collective-permute-start.51 = (bf16[2,256,1408]{2,1,0:T(8,128)(2,1)}, bf16[2,256,1408]{2,1,0:T(8,128)(2,1)}, u32[]{:S(2)}, u32[]{:S(2)}) collective-permute-start(bf16[2,256,1408]{2,1,0:T(8,128)(2,1)} %bitcast.111), channel_id=1, source_target_pairs={{0,72},{64,0},{8,64},{72,8},{1,73},{65,1},{9,65},{73,9},{2,74},{66... | collective-permute-start | bytes 4325384 | tf_op jit(solution)/shard_map/ppermute | solution.py:43
  284.3 82.0 %reduce-scatter.2.cloned.1.call-start = ((), (), s32[]{:S(2)}) async-start(), calls=%async_computation.3 | async-start | bytes 4718592 | tf_op jit(solution)/shard_map/reduce_scatter | solution.py:1023
  318.8 117.5 %all-gather.9.cloned.1.call-start = ((), (), s32[]{:S(2)}) async-start(), calls=%async_computation.4 | async-start | bytes 6488064 | tf_op jit(solution)/shard_map/all_gather | solution.py:821
  344.5 21.8 %collective-permute-start.62 = (bf16[2,120,2048]{2,1,0:T(8,128)(2,1)}, bf16[2,120,2048]{2,1,0:T(8,128)(2,1)}, u32[]{:S(2)}, u32[]{:S(2)}) collective-permute-start(bf16[2,120,2048]{2,1,0:T(8,128)(2,1)} %get-tuple-element.289), channel_id=1, source_target_pairs={{0,64},{64,8},{8,72},{72,0},{1,65},{65,9},{9,73},{73,1},{2,66},{66... | collective-permute-start | bytes 2949128 | tf_op jit(solution)/shard_map/ppermute | solution.py:43
  345.1 21.2 %collective-permute-start.63 = (bf16[2,120,2048]{2,1,0:T(8,128)(2,1)}, bf16[2,120,2048]{2,1,0:T(8,128)(2,1)}, u32[]{:S(2)}, u32[]{:S(2)}) collective-permute-start(bf16[2,120,2048]{2,1,0:T(8,128)(2,1)} %get-tuple-element.290), channel_id=1, source_target_pairs={{0,72},{64,0},{8,64},{72,8},{1,73},{65,1},{9,65},{73,9},{2,74},{66... | collective-permute-start | bytes 2949128 | tf_op jit(solution)/shard_map/ppermute | solution.py:43
  366.3 131.0 %all-gather.11.cloned.1.call-start = ((), (), s32[]{:S(2)}) async-start(), calls=%async_computation.5 | async-start | bytes 4423680 | tf_op jit(solution)/shard_map/all_gather | solution.py:821
  392.9 23.1 %collective-permute-start.69 = (bf16[120,2048]{1,0:T(8,128)(2,1)}, bf16[120,2048]{1,0:T(8,128)(2,1)}, u32[]{:S(2)}, u32[]{:S(2)}) collective-permute-start(bf16[120,2048]{1,0:T(8,128)(2,1)} %get-tuple-element.355), channel_id=1, source_target_pairs={{0,16},{16,32},{32,48},{48,0},{1,17},{17,33},{33,49},{49,1},{2,18}... | collective-permute-start | bytes 1474568 | tf_op jit(solution)/shard_map/ppermute | solution.py:45
  392.9 25.6 %collective-permute-start.70 = (bf16[120,2048]{1,0:T(8,128)(2,1)}, bf16[120,2048]{1,0:T(8,128)(2,1)}, u32[]{:S(2)}, u32[]{:S(2)}) collective-permute-start(bf16[120,2048]{1,0:T(8,128)(2,1)} %get-tuple-element.354), channel_id=1, source_target_pairs={{0,32},{16,48},{32,0},{48,16},{1,33},{17,49},{33,1},{49,17},{2,34}... | collective-permute-start | bytes 1474568 | tf_op jit(solution)/shard_map/ppermute | solution.py:45
  396.4 22.1 %collective-permute-start.71 = (bf16[120,2048]{1,0:T(8,128)(2,1)}, bf16[120,2048]{1,0:T(8,128)(2,1)}, u32[]{:S(2)}, u32[]{:S(2)}) collective-permute-start(bf16[120,2048]{1,0:T(8,128)(2,1)} %get-tuple-element.353), channel_id=1, source_target_pairs={{0,48},{16,0},{32,16},{48,32},{1,49},{17,1},{33,17},{49,33},{2,50}... | collective-permute-start | bytes 1474568 | tf_op jit(solution)/shard_map/ppermute | solution.py:45
  455.4 27.7 %collective-permute-start.82 = (bf16[256,320]{1,0:T(8,128)(2,1)S(1)}, bf16[256,320]{1,0:T(8,128)(2,1)S(1)}, u32[]{:S(2)}, u32[]{:S(2)}) collective-permute-start(bf16[256,320]{1,0:T(8,128)(2,1)S(1)} %add_convert_fusion.11.refs_0_), channel_id=1, source_target_pairs={{0,6},{2,0},{4,2},{6,4},{1,7},{3,1},{5,3},{7,5},{8,14},{10,8},{12,... | collective-permute-start | bytes 491528 | tf_op jit(solution)/shard_map/ppermute | solution.py:45
  (182 other events, 1985.2 us)
Sparse Core Ops, SparseCore 0:
  137.3 38.7 all-gather.4
  284.4 37.6 all-gather.6
  325.1 35.2 reduce-scatter.1
  366.4 43.2 all-gather.8
  455.4 41.7 all-gather.10
where the time goes:
time: 519 us; the launch traced here: 510 us
  starting transfers between devices  133 us (26%)
  waiting for transfers between devices  124 us (24%)
  matrix products  62.6 us (12%)
  local copies, waits for them, and re-layouts  58.9 us (11%)
  Pallas kernels  58.9 us (11%)
  other arithmetic  55.8 us (11%)
  between operations  17.7 us (3%)
    ppermute x71, starting transfers between devices, ring(): lax.ppermute(values, axis, [(i, (i + step) % count) for i in range(count)])  104 us
    ppermute x71, waiting for transfers between devices, ring(): lax.ppermute(values, axis, [(i, (i + step) % count) for i in range(count)])  75.5 us
    dot_general x15, matrix products, contract(): return jnp.einsum(form, left, right, preferred_element_type=F32)  62.6 us
    unnamed x232, local copies, waits for them, and re-layouts  31.2 us
    ppermute x14, waiting for transfers between devices, ring(): lax.ppermute(values, axis, [(spot[z], spot[(z + step) % 4]) for z in rang...  29.3 us
    ppermute x14, starting transfers between devices, ring(): lax.ppermute(values, axis, [(spot[z], spot[(z + step) % 4]) for z in rang...  18 us
    pallas_call x6, Pallas kernels, put_in_place(): pl.pallas_call(functools.partial(place_kernel, copies), grid_spec=pltpu.P...  16.4 us
    pallas_call x2, Pallas kernels, attend_back(): pl.pallas_call(functools.partial(backward_kernel, begin=begin), grid_spec...  11.7 us
  transfers between devices with their start and end apart: 94, of which 35 were waited for; matrix products, arithmetic and copies ran while one was open for 23% of the time, Pallas kernels for 9%

commit v1 on v0

--- a/solution.py
+++ b/solution.py
@@ -910,9 +910,9 @@
     keys_t = jnp.where(is_key, mine, theirs)
     values_t = jnp.where(is_key, theirs, mine)
     out_blocks = (out_here, *out_near, *out_far)
-    out_z = across_z(*out_blocks)
     gate_up_pair = jnp.concatenate([gate_up_here, *gate_up_other])
     gate_up_near = near(gate_up_pair, "y")
+    out_z = across_z(*out_blocks)
     attended = attend(meta, query_t, keys_t, values_t)
     (attn_t, mixed_t, lse), out_z, gate_up_near = join(attended, out_z, gate_up_near)
     mixed_parts = exchange_x(mixed_t.reshape(4, 2, Q_OWN, TOK), x)
@@ -1003,7 +1003,9 @@
     )
     grad_here = grad_residual.astype(BF16)
     grad_theirs = ring(grad_here, "core", 1)
-    grad_theirs, grad_here = join(grad_theirs, grad_here)
+    grad_theirs, grad_here, gate_up_mine, gate_up_z = join(
+        grad_theirs, grad_here, gate_up_mine, gate_up_z
+    )
     grad_both = jnp.stack(
         [jnp.where(core == 0, grad_here, grad_theirs), jnp.where(core == 0, grad_theirs, grad_here)]
     )

time: 519 us -> 515 us (level)
    unnamed x232 -> x234, local copies, waits for them, and re-layouts: 31.2 us -> 31.3 us
where the time goes in v1:
time: 515 us; the launch traced here: 506 us
  starting transfers between devices  132 us (26%)
  waiting for transfers between devices  120 us (23%)
  matrix products  62.4 us (12%)
  local copies, waits for them, and re-layouts  59 us (11%)
  Pallas kernels  58.9 us (11%)
  other arithmetic  56.2 us (11%)
  between operations  17.7 us (3%)
    ppermute x71, starting transfers between devices, ring(): lax.ppermute(values, axis, [(i, (i + step) % count) for i in range(count)])  103 us
    ppermute x71, waiting for transfers between devices, ring(): lax.ppermute(values, axis, [(i, (i + step) % count) for i in range(count)])  72 us
    dot_general x15, matrix products, contract(): return jnp.einsum(form, left, right, preferred_element_type=F32)  62.4 us
    unnamed x234, local copies, waits for them, and re-layouts  31.3 us
    ppermute x14, waiting for transfers between devices, ring(): lax.ppermute(values, axis, [(spot[z], spot[(z + step) % 4]) for z in rang...  28.6 us
    ppermute x14, starting transfers between devices, ring(): lax.ppermute(values, axis, [(spot[z], spot[(z + step) % 4]) for z in rang...  18.1 us
    pallas_call x6, Pallas kernels, put_in_place(): pl.pallas_call(functools.partial(place_kernel, copies), grid_spec=pltpu.P...  16.4 us
    pallas_call x2, Pallas kernels, attend_back(): pl.pallas_call(functools.partial(backward_kernel, begin=begin), grid_spec...  11.7 us
  transfers between devices with their start and end apart: 94, of which 35 were waited for; matrix products, arithmetic and copies ran while one was open for 23% of the time, Pallas kernels for 9%

profile of v1, /device:TPU:1, one launch (start us, length us, event | category | flops | bytes accessed | tf_op | source)
XLA Modules:
  0.0 506.3 jit_solution(13597849130826469511)
XLA Ops:
  93.6 7.3 %attend.1 = (f32[8,256,128]{2,1,0:T(8,128)S(1)}, bf16[8,256,128]{2,1,0:T(8,128)(2,1)S(1)}, f32[64,512]{1,0:T(8,128)S(1)}) custom-call(s32[2]{0:T(128)S(1)} %pad_add_fusion.meta, bf16[256,1024]{1,0:T(8,128)(2,1)S(1)} %bitcast.305, bf16[64,2048]{1,0:T(8,128)(2,1)S(1)} %get-tuple-element.410.kt_ref, bf16[64,2048]{1,0:T(8,128)(2,1)S(1)} %get-tuple-element.409.vt_ref), custom_call_target="tpu_custom_call" | custom-call | flops 1000000000 | bytes 3000000 | tf_op jit(solution)/shard_map/attend/pallas_call | solution.py:513
  101.6 7.9 %collective-permute-done.22 = bf16[512,1024]{1,0:T(8,128)(2,1)} collective-permute-done((bf16[512,1024]{1,0:T(8,128)(2,1)}, bf16[512,1024]{1,0:T(8,128)(2,1)}, u32[]{:S(2)}, u32[]{:S(2)}) %collective-permute-start.22) | collective-permute-done | bytes 1048608 | tf_op jit(solution)/shard_map/ppermute | solution.py:43
  143.9 10.8 %collective-permute-done.35 = bf16[256,1408]{1,0:T(8,128)(2,1)S(1)} collective-permute-done((bf16[256,1408]{1,0:T(8,128)(2,1)S(1)}, bf16[256,1408]{1,0:T(8,128)(2,1)S(1)}, u32[]{:S(2)}, u32[]{:S(2)}) %collective-permute-start.35) | collective-permute-done | bytes 720928 | tf_op jit(solution)/shard_map/ppermute | solution.py:45
  177.1 4.7 put_in_place.9
  193.3 10.4 %fusion.98 = f32[1024,1408]{1,0:T(8,128)S(1)} fusion(bf16[1024,2048]{1,0:T(8,128)(2,1)} %all-gather.5.cloned.1.call-done, bf16[2048,1408]{1,0:T(8,128)(2,1)} %bitcast.291), kind=kOutput, calls=%fused_computation.261 | convolution fusion | flops 5905580032 | bytes 15728640 | tf_op jit(solution)/shard_map/td,df->tf/dot_general | solution.py:799
  209.7 5.4 %multiply_convert_fusion.2 = (bf16[1024,704]{1,0:T(8,128)(2,1)S(1)}, bf16[1024,704]{1,0:T(8,128)(2,1)S(1)}, bf16[1024,704]{1,0:T(8,128)(2,1)}) fusion(f32[1024,1408]{1,0:T(8,128)S(1)} %fusion.98, bf16[1024,2048]{1,0:T(8,128)(2,1)S(1)} %bitcast.296, bf16[704,2048]{1,0:T(8,128)(2,1)S(1)} %bitcast.303), kind=kOutput, calls=%fused_computation.26 | convolution fusion | flops 2963603456 | bytes 17170432 | tf_op jit(solution)/shard_map/td,fd->tf/dot_general | solution.py:799
  216.1 6.9 %convolution_convert_fusion.2 = bf16[1024,2048]{1,0:T(8,128)(2,1)S(1)} fusion(bf16[1024,1408]{1,0:T(8,128)(2,1)S(1)} %pad_maximum_fusion, bf16[2048,1408]{1,0:T(8,128)(2,1)S(1)} %bitcast.294), kind=kOutput, calls=%fused_computation.20 | convolution fusion | flops 5907677184 | bytes 12845056 | tf_op jit(solution)/shard_map/tf,df->td/dot_general | solution.py:799
  225.7 5.9 %convolution_convert_fusion.4 = bf16[1024,1408]{1,0:T(8,128)(2,1)S(1)} fusion(bf16[1024,1408]{1,0:T(8,128)(2,1)} %copy-done.87, bf16[1024,2048]{1,0:T(8,128)(2,1)} %all-gather.5.cloned.1.call-done, s32[]{:T(128)S(6)} %select_n.522), kind=kOutput, calls=%fused_computation.22 | convolution fusion | flops 2954231808 | bytes 7864324 | tf_op jit(solution)/shard_map/td,tf->df/dot_general | solution.py:799
  243.9 4.9 convolution_convert_fusion.1
  248.9 7.6 %convolution_convert_fusion.5 = bf16[704,2048]{1,0:T(8,128)(2,1)} fusion(bf16[1024,704]{1,0:T(8,128)(2,1)} %get-tuple-element.257, bf16[1024,2048]{1,0:T(8,128)(2,1)} %bitcast.297), kind=kOutput, calls=%fused_computation.23 | convolution fusion | flops 2954231808 | bytes 8519680 | tf_op jit(solution)/shard_map/tf,td->fd/dot_general | solution.py:799
  256.5 4.9 convolution_convert_fusion.3
  264.4 10.4 %collective-permute-done.50 = bf16[2,256,1408]{2,1,0:T(8,128)(2,1)S(1)} collective-permute-done((bf16[2,256,1408]{2,1,0:T(8,128)(2,1)}, bf16[2,256,1408]{2,1,0:T(8,128)(2,1)S(1)}, u32[]{:S(2)}, u32[]{:S(2)}) %collective-permute-start.50) | collective-permute-done | bytes 1441824 | tf_op jit(solution)/shard_map/ppermute | solution.py:43
  309.5 5.9 %collective-permute-done.57.refs_2_ = bf16[2,256,128]{2,1,0:T(8,128)(2,1)S(1)} collective-permute-done((bf16[2,256,128]{2,1,0:T(8,128)(2,1)S(1)}, bf16[2,256,128]{2,1,0:T(8,128)(2,1)S(1)}, u32[]{:S(2)}, u32[]{:S(2)}) %collective-permute-start.57) | collective-permute-done | bytes 131104 | tf_op jit(solution)/shard_map/ppermute | solution.py:45
  321.5 4.5 attend_back.2
  328.4 7.0 %collective-permute-done.61 = bf16[256,1408]{1,0:T(8,128)(2,1)} collective-permute-done((bf16[256,1408]{1,0:T(8,128)(2,1)}, bf16[256,1408]{1,0:T(8,128)(2,1)}, u32[]{:S(2)}, u32[]{:S(2)}) %collective-permute-start.61) | collective-permute-done | bytes 720928 | tf_op jit(solution)/shard_map/ppermute | solution.py:45
  343.6 7.2 %attend_back.3 = (f32[4,256,128]{2,1,0:T(8,128)S(1)}, f32[64,2048]{1,0:T(8,128)S(1)}, f32[64,2048]{1,0:T(8,128)S(1)}) custom-call(s32[2]{0:T(128)S(1)} %pad_add_fusion.meta, bf16[256,1024]{1,0:T(8,128)(2,1)S(1)} %bitcast.307, bf16[8,256,128]{2,1,0:T(8,128)(2,1)S(1)} %copy-done.47, f32[8,256,128]{2,1,0:T(8,128)S(1)} %copy-done.31, f32[64,512]{1,0:T(8,128)S(1)} %copy-done.59, ...), custom_call_target="tpu_custom_call" | custom-call | flops 1000000000 | bytes 3000000 | tf_op jit(solution)/shard_map/attend_back/pallas_call | solution.py:548
  354.1 7.7 %collective-permute-done.62 = bf16[2,120,2048]{2,1,0:T(8,128)(2,1)} collective-permute-done((bf16[2,120,2048]{2,1,0:T(8,128)(2,1)}, bf16[2,120,2048]{2,1,0:T(8,128)(2,1)}, u32[]{:S(2)}, u32[]{:S(2)}) %collective-permute-start.62) | collective-permute-done | bytes 983072 | tf_op jit(solution)/shard_map/ppermute | solution.py:43
  362.0 4.7 collective-permute-start.64
  369.8 6.3 %collective-permute-done.65 = bf16[64,1024]{1,0:T(8,128)(2,1)S(1)} collective-permute-done((bf16[64,1024]{1,0:T(8,128)(2,1)S(1)}, bf16[64,1024]{1,0:T(8,128)(2,1)S(1)}, u32[]{:S(2)}, u32[]{:S(2)}) %collective-permute-start.65) | collective-permute-done | bytes 131104 | tf_op jit(solution)/shard_map/ppermute | solution.py:1056
  404.5 4.4 convert_add_fusion.1
  443.0 4.9 collective-permute-start.79
  451.9 11.8 %collective-permute-start.82 = (bf16[256,320]{1,0:T(8,128)(2,1)S(1)}, bf16[256,320]{1,0:T(8,128)(2,1)S(1)}, u32[]{:S(2)}, u32[]{:S(2)}) collective-permute-start(bf16[256,320]{1,0:T(8,128)(2,1)S(1)} %add_convert_fusion.11.refs_0_), channel_id=1, source_target_pairs={{0,6},{2,0},{4,2},{6,4},{1,7},{3,1},{5,3},{7,5},{8,14},{10,8},{12,... | collective-permute-start | bytes 491528 | tf_op jit(solution)/shard_map/ppermute | solution.py:45
  469.4 9.2 %gate_up.1 = (f32[256,5632]{1,0:T(8,128)}, f32[256,5632]{1,0:T(8,128)}, f32[256,128]{1,0:T(8,128)S(1)}) custom-call(bf16[8,256,1408]{2,1,0:T(8,128)(2,1)} %bitcast.335, bf16[256,5632]{1,0:T(8,128)(2,1)S(1)} %copy-done.7, bf16[256,5632]{1,0:T(8,128)(2,1)S(1)} %copy-done.9), custom_call_target="tpu_custom_call" | custom-call | flops 1000000000 | bytes 3000000 | tf_op jit(solution)/shard_map/gate_up/pallas_call | solution.py:693
  484.1 9.2 %all-gather.11.cloned.1.call-done.rows = bf16[960,2048]{1,0:T(8,128)(2,1)} async-done(((bf16[120,2048]{1,0:T(8,128)(2,1)}), bf16[960,2048]{1,0:T(8,128)(2,1)}) %all-gather.11.cloned.1.call-update) | async-done | bytes 3932176 | tf_op jit(solution)/shard_map/all_gather | solution.py:821
  (565 shorter events, 318.8 us)
Async XLA Ops:
  7.2 178.9 %all-gather.5.cloned.1.call-start = ((), (), s32[]{:S(2)}) async-start(), calls=%async_computation.1 | async-start | bytes 4718592 | tf_op jit(solution)/shard_map/all_gather | solution.py:821
  47.0 23.9 %collective-permute-start.18 = (bf16[128,1408]{1,0:T(8,128)(2,1)S(1)}, bf16[128,1408]{1,0:T(8,128)(2,1)S(1)}, u32[]{:S(2)}, u32[]{:S(2)}) collective-permute-start(bf16[128,1408]{1,0:T(8,128)(2,1)S(1)} %get-tuple-element.396), channel_id=1, source_target_pairs={{0,64},{64,8},{8,72},{72,0},{1,65},{65,9},{9,73},{73,1},{2,66},{66... | collective-permute-start | bytes 1081352 | tf_op jit(solution)/shard_map/ppermute | solution.py:43
  82.9 31.9 %collective-permute-start.24 = (bf16[512,1408]{1,0:T(8,128)(2,1)}, bf16[512,1408]{1,0:T(8,128)(2,1)S(1)}, u32[]{:S(2)}, u32[]{:S(2)}) collective-permute-start(bf16[512,1408]{1,0:T(8,128)(2,1)} %constant_dynamic-update-slice_fusion.4), channel_id=1, source_target_pairs={{0,48},{16,0},{32,16},{48,32},{1,49},{17,1},{33,17},{49,33},{2,50}... | collective-permute-start | bytes 4325384 | tf_op jit(solution)/shard_map/ppermute | solution.py:45
  83.3 33.1 %collective-permute-start.25 = (bf16[512,1408]{1,0:T(8,128)(2,1)}, bf16[512,1408]{1,0:T(8,128)(2,1)}, u32[]{:S(2)}, u32[]{:S(2)}) collective-permute-start(bf16[512,1408]{1,0:T(8,128)(2,1)} %constant_dynamic-update-slice_fusion.4), channel_id=1, source_target_pairs={{0,16},{16,32},{32,48},{48,0},{1,17},{17,33},{33,49},{49,1},{2,18}... | collective-permute-start | bytes 4325384 | tf_op jit(solution)/shard_map/ppermute | solution.py:45
  85.4 24.1 %collective-permute-start.22 = (bf16[512,1024]{1,0:T(8,128)(2,1)}, bf16[512,1024]{1,0:T(8,128)(2,1)}, u32[]{:S(2)}, u32[]{:S(2)}) collective-permute-start(bf16[512,1024]{1,0:T(8,128)(2,1)} %pad_maximum_fusion.2), channel_id=1, source_target_pairs={{0,64},{64,8},{8,72},{72,0},{1,65},{65,9},{9,73},{73,1},{2,66},{66... | collective-permute-start | bytes 3145736 | tf_op jit(solution)/shard_map/ppermute | solution.py:43
  87.2 23.2 %collective-permute-start.23 = (bf16[512,1024]{1,0:T(8,128)(2,1)}, bf16[512,1024]{1,0:T(8,128)(2,1)}, u32[]{:S(2)}, u32[]{:S(2)}) collective-permute-start(bf16[512,1024]{1,0:T(8,128)(2,1)} %pad_maximum_fusion.3), channel_id=1, source_target_pairs={{0,72},{64,0},{8,64},{72,8},{1,73},{65,1},{9,65},{73,9},{2,74},{66... | collective-permute-start | bytes 3145736 | tf_op jit(solution)/shard_map/ppermute | solution.py:43
  137.2 198.2 %all-gather.7.cloned.1.call-start = ((), (), s32[]{:S(2)}) async-start(), calls=%async_computation.2 | async-start | bytes 4718592 | tf_op jit(solution)/shard_map/all_gather | solution.py:821
  140.1 22.0 %collective-permute-start.33 = (bf16[128,2048]{1,0:T(8,128)(2,1)}, bf16[128,2048]{1,0:T(8,128)(2,1)S(1)}, u32[]{:S(2)}, u32[]{:S(2)}) collective-permute-start(bf16[128,2048]{1,0:T(8,128)(2,1)} %param.14), channel_id=1, source_target_pairs={{0,6},{2,0},{4,2},{6,4},{1,7},{3,1},{5,3},{7,5},{8,14},{10,8},{12,... | collective-permute-start | bytes 1572872 | tf_op jit(solution)/shard_map/ppermute | solution.py:45
  142.0 24.4 %collective-permute-start.34 = (bf16[128,2048]{1,0:T(8,128)(2,1)}, bf16[128,2048]{1,0:T(8,128)(2,1)S(1)}, u32[]{:S(2)}, u32[]{:S(2)}) collective-permute-start(bf16[128,2048]{1,0:T(8,128)(2,1)} %param.14), channel_id=1, source_target_pairs={{0,2},{2,4},{4,6},{6,0},{1,3},{3,5},{5,7},{7,1},{8,10},{10,12},{12... | collective-permute-start | bytes 1572872 | tf_op jit(solution)/shard_map/ppermute | solution.py:45
  169.7 34.1 %collective-permute-start.43 = (bf16[128,2048]{1,0:T(8,128)(2,1)}, bf16[128,2048]{1,0:T(8,128)(2,1)}, u32[]{:S(2)}, u32[]{:S(2)}) collective-permute-start(bf16[128,2048]{1,0:T(8,128)(2,1)} %param.14), channel_id=1, source_target_pairs={{0,1},{1,0},{2,3},{3,2},{4,5},{5,4},{6,7},{7,6},{8,9},{9,8},{10,11... | collective-permute-start | bytes 1572872 | tf_op jit(solution)/shard_map/ppermute | solution.py:45
  238.6 25.8 %collective-permute-start.47 = (bf16[128,2048]{1,0:T(8,128)(2,1)}, bf16[128,2048]{1,0:T(8,128)(2,1)}, u32[]{:S(2)}, u32[]{:S(2)}) collective-permute-start(bf16[128,2048]{1,0:T(8,128)(2,1)} %get-tuple-element.374), channel_id=1, source_target_pairs={{0,2},{2,4},{4,6},{6,0},{1,3},{3,5},{5,7},{7,1},{8,10},{10,12},{12... | collective-permute-start | bytes 1572872 | tf_op jit(solution)/shard_map/ppermute | solution.py:45
  238.6 25.8 %collective-permute-start.48 = (bf16[128,2048]{1,0:T(8,128)(2,1)}, bf16[128,2048]{1,0:T(8,128)(2,1)}, u32[]{:S(2)}, u32[]{:S(2)}) collective-permute-start(bf16[128,2048]{1,0:T(8,128)(2,1)} %get-tuple-element.373), channel_id=1, source_target_pairs={{0,6},{2,0},{4,2},{6,4},{1,7},{3,1},{5,3},{7,5},{8,14},{10,8},{12,... | collective-permute-start | bytes 1572872 | tf_op jit(solution)/shard_map/ppermute | solution.py:45
  241.2 23.1 %collective-permute-start.49 = (bf16[128,2048]{1,0:T(8,128)(2,1)}, bf16[128,2048]{1,0:T(8,128)(2,1)}, u32[]{:S(2)}, u32[]{:S(2)}) collective-permute-start(bf16[128,2048]{1,0:T(8,128)(2,1)} %get-tuple-element.372), channel_id=1, source_target_pairs={{0,4},{2,6},{4,0},{6,2},{1,5},{3,7},{5,1},{7,3},{8,12},{10,14},{12... | collective-permute-start | bytes 1572872 | tf_op jit(solution)/shard_map/ppermute | solution.py:45
  241.2 33.5 %collective-permute-start.50 = (bf16[2,256,1408]{2,1,0:T(8,128)(2,1)}, bf16[2,256,1408]{2,1,0:T(8,128)(2,1)S(1)}, u32[]{:S(2)}, u32[]{:S(2)}) collective-permute-start(bf16[2,256,1408]{2,1,0:T(8,128)(2,1)} %bitcast.110), channel_id=1, source_target_pairs={{0,64},{64,8},{8,72},{72,0},{1,65},{65,9},{9,73},{73,1},{2,66},{66... | collective-permute-start | bytes 4325384 | tf_op jit(solution)/shard_map/ppermute | solution.py:43
  241.2 33.5 %collective-permute-start.51 = (bf16[2,256,1408]{2,1,0:T(8,128)(2,1)}, bf16[2,256,1408]{2,1,0:T(8,128)(2,1)}, u32[]{:S(2)}, u32[]{:S(2)}) collective-permute-start(bf16[2,256,1408]{2,1,0:T(8,128)(2,1)} %bitcast.111), channel_id=1, source_target_pairs={{0,72},{64,0},{8,64},{72,8},{1,73},{65,1},{9,65},{73,9},{2,74},{66... | collective-permute-start | bytes 4325384 | tf_op jit(solution)/shard_map/ppermute | solution.py:43
  284.3 77.5 %reduce-scatter.2.cloned.1.call-start = ((), (), s32[]{:S(2)}) async-start(), calls=%async_computation.3 | async-start | bytes 4718592 | tf_op jit(solution)/shard_map/reduce_scatter | solution.py:1025
  315.7 117.1 %all-gather.9.cloned.1.call-start = ((), (), s32[]{:S(2)}) async-start(), calls=%async_computation.4 | async-start | bytes 6488064 | tf_op jit(solution)/shard_map/all_gather | solution.py:821
  340.6 21.2 %collective-permute-start.62 = (bf16[2,120,2048]{2,1,0:T(8,128)(2,1)}, bf16[2,120,2048]{2,1,0:T(8,128)(2,1)}, u32[]{:S(2)}, u32[]{:S(2)}) collective-permute-start(bf16[2,120,2048]{2,1,0:T(8,128)(2,1)} %get-tuple-element.295), channel_id=1, source_target_pairs={{0,64},{64,8},{8,72},{72,0},{1,65},{65,9},{9,73},{73,1},{2,66},{66... | collective-permute-start | bytes 2949128 | tf_op jit(solution)/shard_map/ppermute | solution.py:43
  341.3 20.5 %collective-permute-start.63 = (bf16[2,120,2048]{2,1,0:T(8,128)(2,1)}, bf16[2,120,2048]{2,1,0:T(8,128)(2,1)}, u32[]{:S(2)}, u32[]{:S(2)}) collective-permute-start(bf16[2,120,2048]{2,1,0:T(8,128)(2,1)} %get-tuple-element.296), channel_id=1, source_target_pairs={{0,72},{64,0},{8,64},{72,8},{1,73},{65,1},{9,65},{73,9},{2,74},{66... | collective-permute-start | bytes 2949128 | tf_op jit(solution)/shard_map/ppermute | solution.py:43
  361.8 131.4 %all-gather.11.cloned.1.call-start = ((), (), s32[]{:S(2)}) async-start(), calls=%async_computation.5 | async-start | bytes 4423680 | tf_op jit(solution)/shard_map/all_gather | solution.py:821
  388.7 23.5 %collective-permute-start.69 = (bf16[120,2048]{1,0:T(8,128)(2,1)}, bf16[120,2048]{1,0:T(8,128)(2,1)}, u32[]{:S(2)}, u32[]{:S(2)}) collective-permute-start(bf16[120,2048]{1,0:T(8,128)(2,1)} %get-tuple-element.361), channel_id=1, source_target_pairs={{0,16},{16,32},{32,48},{48,0},{1,17},{17,33},{33,49},{49,1},{2,18}... | collective-permute-start | bytes 1474568 | tf_op jit(solution)/shard_map/ppermute | solution.py:45
  389.2 25.7 %collective-permute-start.70 = (bf16[120,2048]{1,0:T(8,128)(2,1)}, bf16[120,2048]{1,0:T(8,128)(2,1)}, u32[]{:S(2)}, u32[]{:S(2)}) collective-permute-start(bf16[120,2048]{1,0:T(8,128)(2,1)} %get-tuple-element.360), channel_id=1, source_target_pairs={{0,32},{16,48},{32,0},{48,16},{1,33},{17,49},{33,1},{49,17},{2,34}... | collective-permute-start | bytes 1474568 | tf_op jit(solution)/shard_map/ppermute | solution.py:45
  392.6 22.2 %collective-permute-start.71 = (bf16[120,2048]{1,0:T(8,128)(2,1)}, bf16[120,2048]{1,0:T(8,128)(2,1)}, u32[]{:S(2)}, u32[]{:S(2)}) collective-permute-start(bf16[120,2048]{1,0:T(8,128)(2,1)} %get-tuple-element.359), channel_id=1, source_target_pairs={{0,48},{16,0},{32,16},{48,32},{1,49},{17,1},{33,17},{49,33},{2,50}... | collective-permute-start | bytes 1474568 | tf_op jit(solution)/shard_map/ppermute | solution.py:45
  451.9 26.8 %collective-permute-start.82 = (bf16[256,320]{1,0:T(8,128)(2,1)S(1)}, bf16[256,320]{1,0:T(8,128)(2,1)S(1)}, u32[]{:S(2)}, u32[]{:S(2)}) collective-permute-start(bf16[256,320]{1,0:T(8,128)(2,1)S(1)} %add_convert_fusion.11.refs_0_), channel_id=1, source_target_pairs={{0,6},{2,0},{4,2},{6,4},{1,7},{3,1},{5,3},{7,5},{8,14},{10,8},{12,... | collective-permute-start | bytes 491528 | tf_op jit(solution)/shard_map/ppermute | solution.py:45
  (183 other events, 1981.5 us)
Sparse Core Ops, SparseCore 0:
  137.3 38.7 all-gather.4
  284.4 37.7 all-gather.6
  325.1 34.7 reduce-scatter.1
  361.9 44.4 all-gather.8
  451.9 41.2 all-gather.10

commit v2 on v1

--- a/solution.py
+++ b/solution.py
@@ -419,19 +419,40 @@
         v_ref[HEAD_DIM:, :] = jnp.where(row == 0, 1.0, 0.0).astype(BF16)
 
     query = heads_side_by_side(q_ref[...])
-    top_ref[...] = jnp.full_like(top_ref, NEG_LARGE)
-    acc_ref[...] = jnp.zeros_like(acc_ref)
-
-    def step(start, size, masked):
+    chunks = HALF // KEY_CHUNK
+    final = j == GROUP - 1
+    every = tuple(range(chunks))
+
+    def scores_of(start, size, masked):
         rows = slice(start, start + size)
-        scores = mask_scores(dot_kn(k_ref[rows, :], query), meta, j, start, masked)
-        old = top_ref[...]
-        new = jnp.maximum(old, jnp.max(scores, axis=0, keepdims=True))
-        weights = jnp.exp(scores - new).astype(BF16)
-        acc_ref[...] = acc_ref[...] * jnp.exp(old - new) + dot_kn(v_ref[:, rows], weights)
-        top_ref[...] = new
-
-    for_visible_keys(meta, j, step)
+        return mask_scores(dot_kn(k_ref[rows, :], query), meta, j, start, masked)
+
+    def finish(parts):
+        top = functools.reduce(
+            jnp.maximum, [jnp.max(scores, axis=0, keepdims=True) for _, scores in parts]
+        )
+        acc = 0.0
+        for start, scores in parts:
+            rows = slice(start, start + scores.shape[0])
+            acc = acc + dot_kn(v_ref[:, rows], jnp.exp(scores - top).astype(BF16))
+        acc_ref[...] = acc
+        top_ref[...] = top
+
+    for last in range(chunks + 1):
+        size = min(last + 1, chunks) * KEY_CHUNK
+        whole_mask = last == chunks
+        here = final if whole_mask else (j * TOK // KEY_CHUNK == last) & jnp.logical_not(final)
+        masked = every if whole_mask else (0, last)
+
+        @pl.when(here & (meta[0] == 1))
+        def _(size=size, masked=masked, whole_mask=whole_mask):
+            earlier = scores_of(0, HALF, every if whole_mask else (0,))
+            finish([(0, earlier), (HALF, scores_of(HALF, size, masked))])
+
+        @pl.when(here & (meta[0] == 0))
+        def _(size=size, masked=masked):
+            finish([(HALF, scores_of(HALF, size, masked))])
+
     total = acc_ref[HEAD_DIM : HEAD_DIM + 1, :]
     attended = heads_stacked(acc_ref[:HEAD_DIM, :] / total)
     out_ref[0] = attended
@@ -987,8 +1008,8 @@
     back_total, gate_up_pairs, hidden, normed_mlp, grad_acts = join(
         back_total, (gate_up_theirs[:2], gate_up_theirs[2:]), hidden, normed_mlp, grad_acts
     )
+    gate_up_z = scatter_z(gate_up_pairs)
     back_rows = rows_along_x(back_total, x)
-    gate_up_z = scatter_z(gate_up_pairs)
     gate_up_mine = gate_up_product(zl * 4, 4)
     part_down = contract("tf,td->fd", hidden, cotangent_all).astype(BF16)
     part_down = part_down.reshape(8, SUB, D)

time: 515 us -> 515 us (level)
  no operation moved by 1% of the time
where the time goes in v2:
time: 515 us; the launch traced here: 507 us
  starting transfers between devices  133 us (26%)
  waiting for transfers between devices  119 us (23%)
  matrix products  62.4 us (12%)
  Pallas kernels  59.2 us (11%)
  local copies, waits for them, and re-layouts  59 us (11%)
  other arithmetic  56.2 us (11%)
  between operations  17.7 us (3%)
    ppermute x71, starting transfers between devices, ring(): lax.ppermute(values, axis, [(i, (i + step) % count) for i in range(count)])  103 us
    ppermute x71, waiting for transfers between devices, ring(): lax.ppermute(values, axis, [(i, (i + step) % count) for i in range(count)])  71.3 us
    dot_general x15, matrix products, contract(): return jnp.einsum(form, left, right, preferred_element_type=F32)  62.4 us
    unnamed x234, local copies, waits for them, and re-layouts  31.3 us
    ppermute x14, waiting for transfers between devices, ring(): lax.ppermute(values, axis, [(spot[z], spot[(z + step) % 4]) for z in rang...  28.5 us
    ppermute x14, starting transfers between devices, ring(): lax.ppermute(values, axis, [(spot[z], spot[(z + step) % 4]) for z in rang...  18.9 us
    pallas_call x6, Pallas kernels, put_in_place(): pl.pallas_call(functools.partial(place_kernel, copies), grid_spec=pltpu.P...  16.4 us
    pallas_call x2, Pallas kernels, attend_back(): pl.pallas_call(functools.partial(backward_kernel, begin=begin), grid_spec...  11.7 us
  transfers between devices with their start and end apart: 94, of which 35 were waited for; matrix products, arithmetic and copies ran while one was open for 23% of the time, Pallas kernels for 9%

profile of v2, /device:TPU:1, one launch (start us, length us, event | category | flops | bytes accessed | tf_op | source)
XLA Modules:
  0.0 506.7 jit_solution(1226449692569880625)
XLA Ops:
  93.6 7.7 %attend.1 = (f32[8,256,128]{2,1,0:T(8,128)S(1)}, bf16[8,256,128]{2,1,0:T(8,128)(2,1)S(1)}, f32[64,512]{1,0:T(8,128)S(1)}) custom-call(s32[2]{0:T(128)S(1)} %pad_add_fusion.meta, bf16[256,1024]{1,0:T(8,128)(2,1)S(1)} %bitcast.305, bf16[64,2048]{1,0:T(8,128)(2,1)S(1)} %get-tuple-element.410.kt_ref, bf16[64,2048]{1,0:T(8,128)(2,1)S(1)} %get-tuple-element.409.vt_ref), custom_call_target="tpu_custom_call" | custom-call | flops 1000000000 | bytes 3000000 | tf_op jit(solution)/shard_map/attend/pallas_call | solution.py:534
  102.0 7.5 %collective-permute-done.22 = bf16[512,1024]{1,0:T(8,128)(2,1)} collective-permute-done((bf16[512,1024]{1,0:T(8,128)(2,1)}, bf16[512,1024]{1,0:T(8,128)(2,1)}, u32[]{:S(2)}, u32[]{:S(2)}) %collective-permute-start.22) | collective-permute-done | bytes 1048608 | tf_op jit(solution)/shard_map/ppermute | solution.py:43
  144.1 10.9 %collective-permute-done.35 = bf16[256,1408]{1,0:T(8,128)(2,1)S(1)} collective-permute-done((bf16[256,1408]{1,0:T(8,128)(2,1)S(1)}, bf16[256,1408]{1,0:T(8,128)(2,1)S(1)}, u32[]{:S(2)}, u32[]{:S(2)}) %collective-permute-start.35) | collective-permute-done | bytes 720928 | tf_op jit(solution)/shard_map/ppermute | solution.py:45
  177.2 4.7 put_in_place.9
  193.7 10.4 %fusion.98 = f32[1024,1408]{1,0:T(8,128)S(1)} fusion(bf16[1024,2048]{1,0:T(8,128)(2,1)} %all-gather.5.cloned.1.call-done, bf16[2048,1408]{1,0:T(8,128)(2,1)} %bitcast.291), kind=kOutput, calls=%fused_computation.261 | convolution fusion | flops 5905580032 | bytes 15728640 | tf_op jit(solution)/shard_map/td,df->tf/dot_general | solution.py:820
  210.1 5.5 %multiply_convert_fusion.2 = (bf16[1024,704]{1,0:T(8,128)(2,1)S(1)}, bf16[1024,704]{1,0:T(8,128)(2,1)S(1)}, bf16[1024,704]{1,0:T(8,128)(2,1)}) fusion(f32[1024,1408]{1,0:T(8,128)S(1)} %fusion.98, bf16[1024,2048]{1,0:T(8,128)(2,1)S(1)} %bitcast.296, bf16[704,2048]{1,0:T(8,128)(2,1)S(1)} %bitcast.303), kind=kOutput, calls=%fused_computation.26 | convolution fusion | flops 2963603456 | bytes 17170432 | tf_op jit(solution)/shard_map/td,fd->tf/dot_general | solution.py:820
  216.5 6.9 %convolution_convert_fusion.2 = bf16[1024,2048]{1,0:T(8,128)(2,1)S(1)} fusion(bf16[1024,1408]{1,0:T(8,128)(2,1)S(1)} %pad_maximum_fusion, bf16[2048,1408]{1,0:T(8,128)(2,1)S(1)} %bitcast.294), kind=kOutput, calls=%fused_computation.20 | convolution fusion | flops 5907677184 | bytes 12845056 | tf_op jit(solution)/shard_map/tf,df->td/dot_general | solution.py:820
  225.7 5.9 %convolution_convert_fusion.4 = bf16[1024,1408]{1,0:T(8,128)(2,1)S(1)} fusion(bf16[1024,1408]{1,0:T(8,128)(2,1)} %copy-done.87, bf16[1024,2048]{1,0:T(8,128)(2,1)} %all-gather.5.cloned.1.call-done, s32[]{:T(128)S(6)} %select_n.522), kind=kOutput, calls=%fused_computation.22 | convolution fusion | flops 2954231808 | bytes 7864324 | tf_op jit(solution)/shard_map/td,tf->df/dot_general | solution.py:820
  244.4 4.9 convolution_convert_fusion.1
  249.3 7.6 %convolution_convert_fusion.5 = bf16[704,2048]{1,0:T(8,128)(2,1)} fusion(bf16[1024,704]{1,0:T(8,128)(2,1)} %get-tuple-element.257, bf16[1024,2048]{1,0:T(8,128)(2,1)} %bitcast.297), kind=kOutput, calls=%fused_computation.23 | convolution fusion | flops 2954231808 | bytes 8519680 | tf_op jit(solution)/shard_map/tf,td->fd/dot_general | solution.py:820
  256.9 4.9 convolution_convert_fusion.3
  264.3 10.4 %collective-permute-done.50 = bf16[2,256,1408]{2,1,0:T(8,128)(2,1)S(1)} collective-permute-done((bf16[2,256,1408]{2,1,0:T(8,128)(2,1)}, bf16[2,256,1408]{2,1,0:T(8,128)(2,1)S(1)}, u32[]{:S(2)}, u32[]{:S(2)}) %collective-permute-start.50) | collective-permute-done | bytes 1441824 | tf_op jit(solution)/shard_map/ppermute | solution.py:43
  309.5 5.9 %collective-permute-done.57.refs_2_ = bf16[2,256,128]{2,1,0:T(8,128)(2,1)S(1)} collective-permute-done((bf16[2,256,128]{2,1,0:T(8,128)(2,1)S(1)}, bf16[2,256,128]{2,1,0:T(8,128)(2,1)S(1)}, u32[]{:S(2)}, u32[]{:S(2)}) %collective-permute-start.57) | collective-permute-done | bytes 131104 | tf_op jit(solution)/shard_map/ppermute | solution.py:45
  322.0 4.5 attend_back.2
  328.8 6.6 %collective-permute-done.61 = bf16[256,1408]{1,0:T(8,128)(2,1)} collective-permute-done((bf16[256,1408]{1,0:T(8,128)(2,1)}, bf16[256,1408]{1,0:T(8,128)(2,1)}, u32[]{:S(2)}, u32[]{:S(2)}) %collective-permute-start.61) | collective-permute-done | bytes 720928 | tf_op jit(solution)/shard_map/ppermute | solution.py:45
  344.0 7.2 %attend_back.3 = (f32[4,256,128]{2,1,0:T(8,128)S(1)}, f32[64,2048]{1,0:T(8,128)S(1)}, f32[64,2048]{1,0:T(8,128)S(1)}) custom-call(s32[2]{0:T(128)S(1)} %pad_add_fusion.meta, bf16[256,1024]{1,0:T(8,128)(2,1)S(1)} %bitcast.307, bf16[8,256,128]{2,1,0:T(8,128)(2,1)S(1)} %copy-done.47, f32[8,256,128]{2,1,0:T(8,128)S(1)} %copy-done.31, f32[64,512]{1,0:T(8,128)S(1)} %copy-done.59, ...), custom_call_target="tpu_custom_call" | custom-call | flops 1000000000 | bytes 3000000 | tf_op jit(solution)/shard_map/attend_back/pallas_call | solution.py:569
  354.5 7.9 %collective-permute-done.62 = bf16[2,120,2048]{2,1,0:T(8,128)(2,1)} collective-permute-done((bf16[2,120,2048]{2,1,0:T(8,128)(2,1)}, bf16[2,120,2048]{2,1,0:T(8,128)(2,1)}, u32[]{:S(2)}, u32[]{:S(2)}) %collective-permute-start.62) | collective-permute-done | bytes 983072 | tf_op jit(solution)/shard_map/ppermute | solution.py:43
  362.6 4.5 collective-permute-start.64
  370.2 6.3 %collective-permute-done.65 = bf16[64,1024]{1,0:T(8,128)(2,1)S(1)} collective-permute-done((bf16[64,1024]{1,0:T(8,128)(2,1)S(1)}, bf16[64,1024]{1,0:T(8,128)(2,1)S(1)}, u32[]{:S(2)}, u32[]{:S(2)}) %collective-permute-start.65) | collective-permute-done | bytes 131104 | tf_op jit(solution)/shard_map/ppermute | solution.py:1077
  405.0 4.4 convert_add_fusion.1
  443.4 4.9 collective-permute-start.79
  452.3 11.7 %collective-permute-start.82 = (bf16[256,320]{1,0:T(8,128)(2,1)S(1)}, bf16[256,320]{1,0:T(8,128)(2,1)S(1)}, u32[]{:S(2)}, u32[]{:S(2)}) collective-permute-start(bf16[256,320]{1,0:T(8,128)(2,1)S(1)} %add_convert_fusion.11.refs_0_), channel_id=1, source_target_pairs={{0,6},{2,0},{4,2},{6,4},{1,7},{3,1},{5,3},{7,5},{8,14},{10,8},{12,... | collective-permute-start | bytes 491528 | tf_op jit(solution)/shard_map/ppermute | solution.py:45
  469.8 9.2 %gate_up.1 = (f32[256,5632]{1,0:T(8,128)}, f32[256,5632]{1,0:T(8,128)}, f32[256,128]{1,0:T(8,128)S(1)}) custom-call(bf16[8,256,1408]{2,1,0:T(8,128)(2,1)} %bitcast.335, bf16[256,5632]{1,0:T(8,128)(2,1)S(1)} %copy-done.7, bf16[256,5632]{1,0:T(8,128)(2,1)S(1)} %copy-done.9), custom_call_target="tpu_custom_call" | custom-call | flops 1000000000 | bytes 3000000 | tf_op jit(solution)/shard_map/gate_up/pallas_call | solution.py:714
  484.5 9.2 %all-gather.11.cloned.1.call-done.rows = bf16[960,2048]{1,0:T(8,128)(2,1)} async-done(((bf16[120,2048]{1,0:T(8,128)(2,1)}), bf16[960,2048]{1,0:T(8,128)(2,1)}) %all-gather.11.cloned.1.call-update) | async-done | bytes 3932176 | tf_op jit(solution)/shard_map/all_gather | solution.py:842
  (565 shorter events, 319.5 us)
Async XLA Ops:
  7.2 178.9 %all-gather.5.cloned.1.call-start = ((), (), s32[]{:S(2)}) async-start(), calls=%async_computation.1 | async-start | bytes 4718592 | tf_op jit(solution)/shard_map/all_gather | solution.py:842
  47.0 23.9 %collective-permute-start.18 = (bf16[128,1408]{1,0:T(8,128)(2,1)S(1)}, bf16[128,1408]{1,0:T(8,128)(2,1)S(1)}, u32[]{:S(2)}, u32[]{:S(2)}) collective-permute-start(bf16[128,1408]{1,0:T(8,128)(2,1)S(1)} %get-tuple-element.396), channel_id=1, source_target_pairs={{0,64},{64,8},{8,72},{72,0},{1,65},{65,9},{9,73},{73,1},{2,66},{66... | collective-permute-start | bytes 1081352 | tf_op jit(solution)/shard_map/ppermute | solution.py:43
  82.9 31.9 %collective-permute-start.24 = (bf16[512,1408]{1,0:T(8,128)(2,1)}, bf16[512,1408]{1,0:T(8,128)(2,1)S(1)}, u32[]{:S(2)}, u32[]{:S(2)}) collective-permute-start(bf16[512,1408]{1,0:T(8,128)(2,1)} %constant_dynamic-update-slice_fusion.4), channel_id=1, source_target_pairs={{0,48},{16,0},{32,16},{48,32},{1,49},{17,1},{33,17},{49,33},{2,50}... | collective-permute-start | bytes 4325384 | tf_op jit(solution)/shard_map/ppermute | solution.py:45
  83.3 33.1 %collective-permute-start.25 = (bf16[512,1408]{1,0:T(8,128)(2,1)}, bf16[512,1408]{1,0:T(8,128)(2,1)}, u32[]{:S(2)}, u32[]{:S(2)}) collective-permute-start(bf16[512,1408]{1,0:T(8,128)(2,1)} %constant_dynamic-update-slice_fusion.4), channel_id=1, source_target_pairs={{0,16},{16,32},{32,48},{48,0},{1,17},{17,33},{33,49},{49,1},{2,18}... | collective-permute-start | bytes 4325384 | tf_op jit(solution)/shard_map/ppermute | solution.py:45
  85.4 24.1 %collective-permute-start.22 = (bf16[512,1024]{1,0:T(8,128)(2,1)}, bf16[512,1024]{1,0:T(8,128)(2,1)}, u32[]{:S(2)}, u32[]{:S(2)}) collective-permute-start(bf16[512,1024]{1,0:T(8,128)(2,1)} %pad_maximum_fusion.2), channel_id=1, source_target_pairs={{0,64},{64,8},{8,72},{72,0},{1,65},{65,9},{9,73},{73,1},{2,66},{66... | collective-permute-start | bytes 3145736 | tf_op jit(solution)/shard_map/ppermute | solution.py:43
  87.2 23.2 %collective-permute-start.23 = (bf16[512,1024]{1,0:T(8,128)(2,1)}, bf16[512,1024]{1,0:T(8,128)(2,1)}, u32[]{:S(2)}, u32[]{:S(2)}) collective-permute-start(bf16[512,1024]{1,0:T(8,128)(2,1)} %pad_maximum_fusion.3), channel_id=1, source_target_pairs={{0,72},{64,0},{8,64},{72,8},{1,73},{65,1},{9,65},{73,9},{2,74},{66... | collective-permute-start | bytes 3145736 | tf_op jit(solution)/shard_map/ppermute | solution.py:43
  137.4 198.1 %all-gather.7.cloned.1.call-start = ((), (), s32[]{:S(2)}) async-start(), calls=%async_computation.2 | async-start | bytes 4718592 | tf_op jit(solution)/shard_map/all_gather | solution.py:842
  140.3 22.1 %collective-permute-start.33 = (bf16[128,2048]{1,0:T(8,128)(2,1)}, bf16[128,2048]{1,0:T(8,128)(2,1)S(1)}, u32[]{:S(2)}, u32[]{:S(2)}) collective-permute-start(bf16[128,2048]{1,0:T(8,128)(2,1)} %param.14), channel_id=1, source_target_pairs={{0,6},{2,0},{4,2},{6,4},{1,7},{3,1},{5,3},{7,5},{8,14},{10,8},{12,... | collective-permute-start | bytes 1572872 | tf_op jit(solution)/shard_map/ppermute | solution.py:45
  142.2 24.5 %collective-permute-start.34 = (bf16[128,2048]{1,0:T(8,128)(2,1)}, bf16[128,2048]{1,0:T(8,128)(2,1)S(1)}, u32[]{:S(2)}, u32[]{:S(2)}) collective-permute-start(bf16[128,2048]{1,0:T(8,128)(2,1)} %param.14), channel_id=1, source_target_pairs={{0,2},{2,4},{4,6},{6,0},{1,3},{3,5},{5,7},{7,1},{8,10},{10,12},{12... | collective-permute-start | bytes 1572872 | tf_op jit(solution)/shard_map/ppermute | solution.py:45
  169.8 34.3 %collective-permute-start.43 = (bf16[128,2048]{1,0:T(8,128)(2,1)}, bf16[128,2048]{1,0:T(8,128)(2,1)}, u32[]{:S(2)}, u32[]{:S(2)}) collective-permute-start(bf16[128,2048]{1,0:T(8,128)(2,1)} %param.14), channel_id=1, source_target_pairs={{0,1},{1,0},{2,3},{3,2},{4,5},{5,4},{6,7},{7,6},{8,9},{9,8},{10,11... | collective-permute-start | bytes 1572872 | tf_op jit(solution)/shard_map/ppermute | solution.py:45
  238.5 25.8 %collective-permute-start.47 = (bf16[128,2048]{1,0:T(8,128)(2,1)}, bf16[128,2048]{1,0:T(8,128)(2,1)}, u32[]{:S(2)}, u32[]{:S(2)}) collective-permute-start(bf16[128,2048]{1,0:T(8,128)(2,1)} %get-tuple-element.374), channel_id=1, source_target_pairs={{0,2},{2,4},{4,6},{6,0},{1,3},{3,5},{5,7},{7,1},{8,10},{10,12},{12... | collective-permute-start | bytes 1572872 | tf_op jit(solution)/shard_map/ppermute | solution.py:45
  238.5 25.8 %collective-permute-start.48 = (bf16[128,2048]{1,0:T(8,128)(2,1)}, bf16[128,2048]{1,0:T(8,128)(2,1)}, u32[]{:S(2)}, u32[]{:S(2)}) collective-permute-start(bf16[128,2048]{1,0:T(8,128)(2,1)} %get-tuple-element.373), channel_id=1, source_target_pairs={{0,6},{2,0},{4,2},{6,4},{1,7},{3,1},{5,3},{7,5},{8,14},{10,8},{12,... | collective-permute-start | bytes 1572872 | tf_op jit(solution)/shard_map/ppermute | solution.py:45
  241.2 23.1 %collective-permute-start.49 = (bf16[128,2048]{1,0:T(8,128)(2,1)}, bf16[128,2048]{1,0:T(8,128)(2,1)}, u32[]{:S(2)}, u32[]{:S(2)}) collective-permute-start(bf16[128,2048]{1,0:T(8,128)(2,1)} %get-tuple-element.372), channel_id=1, source_target_pairs={{0,4},{2,6},{4,0},{6,2},{1,5},{3,7},{5,1},{7,3},{8,12},{10,14},{12... | collective-permute-start | bytes 1572872 | tf_op jit(solution)/shard_map/ppermute | solution.py:45
  241.2 33.5 %collective-permute-start.50 = (bf16[2,256,1408]{2,1,0:T(8,128)(2,1)}, bf16[2,256,1408]{2,1,0:T(8,128)(2,1)S(1)}, u32[]{:S(2)}, u32[]{:S(2)}) collective-permute-start(bf16[2,256,1408]{2,1,0:T(8,128)(2,1)} %bitcast.110), channel_id=1, source_target_pairs={{0,64},{64,8},{8,72},{72,0},{1,65},{65,9},{9,73},{73,1},{2,66},{66... | collective-permute-start | bytes 4325384 | tf_op jit(solution)/shard_map/ppermute | solution.py:43
  241.2 33.5 %collective-permute-start.51 = (bf16[2,256,1408]{2,1,0:T(8,128)(2,1)}, bf16[2,256,1408]{2,1,0:T(8,128)(2,1)}, u32[]{:S(2)}, u32[]{:S(2)}) collective-permute-start(bf16[2,256,1408]{2,1,0:T(8,128)(2,1)} %bitcast.111), channel_id=1, source_target_pairs={{0,72},{64,0},{8,64},{72,8},{1,73},{65,1},{9,65},{73,9},{2,74},{66... | collective-permute-start | bytes 4325384 | tf_op jit(solution)/shard_map/ppermute | solution.py:43
  284.3 78.1 %reduce-scatter.2.cloned.1.call-start = ((), (), s32[]{:S(2)}) async-start(), calls=%async_computation.3 | async-start | bytes 4718592 | tf_op jit(solution)/shard_map/reduce_scatter | solution.py:1046
  315.7 117.5 %all-gather.9.cloned.1.call-start = ((), (), s32[]{:S(2)}) async-start(), calls=%async_computation.4 | async-start | bytes 6488064 | tf_op jit(solution)/shard_map/all_gather | solution.py:842
  340.7 21.7 %collective-permute-start.62 = (bf16[2,120,2048]{2,1,0:T(8,128)(2,1)}, bf16[2,120,2048]{2,1,0:T(8,128)(2,1)}, u32[]{:S(2)}, u32[]{:S(2)}) collective-permute-start(bf16[2,120,2048]{2,1,0:T(8,128)(2,1)} %get-tuple-element.295), channel_id=1, source_target_pairs={{0,64},{64,8},{8,72},{72,0},{1,65},{65,9},{9,73},{73,1},{2,66},{66... | collective-permute-start | bytes 2949128 | tf_op jit(solution)/shard_map/ppermute | solution.py:43
  341.7 20.7 %collective-permute-start.63 = (bf16[2,120,2048]{2,1,0:T(8,128)(2,1)}, bf16[2,120,2048]{2,1,0:T(8,128)(2,1)}, u32[]{:S(2)}, u32[]{:S(2)}) collective-permute-start(bf16[2,120,2048]{2,1,0:T(8,128)(2,1)} %get-tuple-element.296), channel_id=1, source_target_pairs={{0,72},{64,0},{8,64},{72,8},{1,73},{65,1},{9,65},{73,9},{2,74},{66... | collective-permute-start | bytes 2949128 | tf_op jit(solution)/shard_map/ppermute | solution.py:43
  362.4 131.3 %all-gather.11.cloned.1.call-start = ((), (), s32[]{:S(2)}) async-start(), calls=%async_computation.5 | async-start | bytes 4423680 | tf_op jit(solution)/shard_map/all_gather | solution.py:842
  389.1 23.5 %collective-permute-start.69 = (bf16[120,2048]{1,0:T(8,128)(2,1)}, bf16[120,2048]{1,0:T(8,128)(2,1)}, u32[]{:S(2)}, u32[]{:S(2)}) collective-permute-start(bf16[120,2048]{1,0:T(8,128)(2,1)} %get-tuple-element.361), channel_id=1, source_target_pairs={{0,16},{16,32},{32,48},{48,0},{1,17},{17,33},{33,49},{49,1},{2,18}... | collective-permute-start | bytes 1474568 | tf_op jit(solution)/shard_map/ppermute | solution.py:45
  389.6 25.7 %collective-permute-start.70 = (bf16[120,2048]{1,0:T(8,128)(2,1)}, bf16[120,2048]{1,0:T(8,128)(2,1)}, u32[]{:S(2)}, u32[]{:S(2)}) collective-permute-start(bf16[120,2048]{1,0:T(8,128)(2,1)} %get-tuple-element.360), channel_id=1, source_target_pairs={{0,32},{16,48},{32,0},{48,16},{1,33},{17,49},{33,1},{49,17},{2,34}... | collective-permute-start | bytes 1474568 | tf_op jit(solution)/shard_map/ppermute | solution.py:45
  393.1 22.2 %collective-permute-start.71 = (bf16[120,2048]{1,0:T(8,128)(2,1)}, bf16[120,2048]{1,0:T(8,128)(2,1)}, u32[]{:S(2)}, u32[]{:S(2)}) collective-permute-start(bf16[120,2048]{1,0:T(8,128)(2,1)} %get-tuple-element.359), channel_id=1, source_target_pairs={{0,48},{16,0},{32,16},{48,32},{1,49},{17,1},{33,17},{49,33},{2,50}... | collective-permute-start | bytes 1474568 | tf_op jit(solution)/shard_map/ppermute | solution.py:45
  452.3 26.8 %collective-permute-start.82 = (bf16[256,320]{1,0:T(8,128)(2,1)S(1)}, bf16[256,320]{1,0:T(8,128)(2,1)S(1)}, u32[]{:S(2)}, u32[]{:S(2)}) collective-permute-start(bf16[256,320]{1,0:T(8,128)(2,1)S(1)} %add_convert_fusion.11.refs_0_), channel_id=1, source_target_pairs={{0,6},{2,0},{4,2},{6,4},{1,7},{3,1},{5,3},{7,5},{8,14},{10,8},{12,... | collective-permute-start | bytes 491528 | tf_op jit(solution)/shard_map/ppermute | solution.py:45
  (183 other events, 1984.5 us)
Sparse Core Ops, SparseCore 0:
  137.5 38.7 all-gather.4
  284.4 38.1 all-gather.6
  325.6 34.6 reduce-scatter.1
  362.5 44.2 all-gather.8
  452.4 41.2 all-gather.10
